TPU v7x, 128 devices: a whole 4x4x4 slice. The times are simulated.
128 devices in a mesh: dp: 8 (over z, core), seq: 16 (over x, y).
Axes of the slice: x: 4, y: 4, z: 4, core: 2. Of those that a mesh axis runs over, the one named last changes fastest.
Arguments:
- queries: bfloat16 [8, 8192, 4096], P('dp', 'seq')
- latents: bfloat16 [8, 16, 64, 1280], P('dp', 'seq')
- k_weight: bfloat16 [1280, 4096], P(None, 'seq'), may hold values from -0.15625 to 0.15625
- v_weight: bfloat16 [1280, 4096], P(None, 'seq'), may hold values from -0.15625 to 0.15625
- d_context: bfloat16 [8, 8192, 4096], P('dp', 'seq'), may hold values from -6 to 6
- image_pos: int32 [8, 16], P('dp'), may hold values from 0 to 8191, as said below
- image_slot: int32 [8, 16], P('dp'), may hold values from 0 to 15, each once within a row
Outputs:
- context: bfloat16 [8, 8192, 4096], P('dp', 'seq')
- d_queries: bfloat16 [8, 8192, 4096], P('dp', 'seq')
- d_latents: bfloat16 [8, 16, 64, 1280], P('dp', 'seq')
- d_k_weight: float32 [1280, 4096], P(None, 'seq')
- d_v_weight: float32 [1280, 4096], P(None, 'seq')
Inputs may be any that keep to these rules, and one draw needn't show every extreme that they name: `image_pos`: in every document the image positions rise strictly and the first is 0. The 512 tokens of one seq device attend to at most 3 images, and in every document some device attends to exactly that many. `image_slot`: each row names every slot once.
All inputs are finite; a program needn't handle non-finite values.
Results may differ from a plain program's by a relative error of at most 0.02.
Values may be sent and summed in bfloat16 or wider, within the bound.
A program may use at most 128 MiB of HBM per device.

v0:
```python
import math

import jax
import jax.numpy as jnp
from jax import lax
from jax.sharding import PartitionSpec as P

HD = 128
LATENTS = 64
NEED = 3


EPSILON = 1e-06


def unit_rms(raw_values):
    inverse = lax.rsqrt(jnp.mean(raw_values * raw_values, axis=-1, keepdims=True) + EPSILON)
    return (raw_values * inverse, inverse)


def unit_rms_back(unit_value, inverse, grad_unit):
    return inverse * (
        grad_unit - unit_value * jnp.mean(grad_unit * unit_value, axis=-1, keepdims=True)
    )


def attend(query_raw, cotangent, local_image, keys_need, values_need):
    score_scale = 1.0 / math.sqrt(HD)
    need_count = keys_need.shape[0]
    query_unit, query_inverse = unit_rms(query_raw.astype(jnp.float32))
    query_b = query_unit.astype(jnp.bfloat16)
    select = (local_image[:, None] == jnp.arange(need_count, dtype=jnp.int32)[None, :]).astype(
        jnp.float32
    )
    select_b = select.astype(jnp.bfloat16)
    scores_wide = jnp.einsum(
        "thd,jlhd->thjl", query_b, keys_need, preferred_element_type=jnp.float32
    )
    scores = jnp.sum(scores_wide * select[:, None, :, None], axis=2) * score_scale
    exponent = jnp.exp(scores)
    probability = exponent / jnp.sum(exponent, axis=-1, keepdims=True)
    probs_b = probability.astype(jnp.bfloat16)
    probs_wide = probs_b[:, :, None, :] * select_b[:, None, :, None]
    context = jnp.einsum(
        "thjl,jlhd->thd", probs_wide, values_need, preferred_element_type=jnp.float32
    )
    context = context.astype(jnp.bfloat16)
    dprob_wide = jnp.einsum(
        "thd,jlhd->thjl", cotangent, values_need, preferred_element_type=jnp.float32
    )
    dprob = jnp.sum(dprob_wide * select[:, None, :, None], axis=2)
    dscore = (
        probability * (dprob - jnp.sum(probability * dprob, axis=-1, keepdims=True)) * score_scale
    )
    dscore_b = dscore.astype(jnp.bfloat16)
    dscore_wide = dscore_b[:, :, None, :] * select_b[:, None, :, None]
    query_cot = jnp.einsum(
        "thjl,jlhd->thd", dscore_wide, keys_need, preferred_element_type=jnp.float32
    )
    d_queries = unit_rms_back(query_unit, query_inverse, query_cot).astype(jnp.bfloat16)
    key_part = jnp.einsum(
        "thjl,thd->jlhd", dscore_wide, query_b, preferred_element_type=jnp.float32
    )
    value_part = jnp.einsum(
        "thjl,thd->jlhd", probs_wide, cotangent, preferred_element_type=jnp.float32
    )
    return (context, d_queries, key_part.astype(jnp.bfloat16), value_part.astype(jnp.bfloat16))


def local(queries, latents, k_weight, v_weight, d_context, image_pos, image_slot):
    seq_count = lax.axis_size("seq")
    seq_index = lax.axis_index("seq")
    tokens_dev = queries.shape[1]
    width = queries.shape[2]
    heads_all = width // HD
    cols_dev = k_weight.shape[1]
    heads_dev = cols_dev // HD
    image_count = image_pos.shape[1]
    model_in = latents.shape[3]
    positions = image_pos[0]
    slot_table = image_slot[0]
    block_starts = jnp.arange(seq_count, dtype=jnp.int32) * tokens_dev
    first_images = (
        jnp.sum((positions[None, :] <= block_starts[:, None]).astype(jnp.int32), axis=1) - 1
    )
    needed = jnp.minimum(
        first_images[:, None] + jnp.arange(NEED, dtype=jnp.int32)[None, :], image_count - 1
    )
    needed_slots = slot_table[needed].reshape(-1)
    my_first = first_images[seq_index]
    token_ids = seq_index * tokens_dev + jnp.arange(tokens_dev, dtype=jnp.int32)
    visible = jnp.sum((positions[None, :] <= token_ids[:, None]).astype(jnp.int32), axis=1) - 1
    local_image = visible - my_first
    gathered = lax.all_gather(latents[0], "seq", axis=0, tiled=True)
    flat_slots = gathered.reshape(image_count * LATENTS, model_in)
    keys_raw = jnp.dot(flat_slots, k_weight, preferred_element_type=jnp.float32)
    keys_raw = keys_raw.reshape(image_count, LATENTS, heads_dev, HD)
    key_unit, key_inverse = unit_rms(keys_raw)
    my_slots = lax.dynamic_slice_in_dim(needed_slots, seq_index * NEED, NEED, 0)
    chosen = gathered[my_slots].reshape(NEED * LATENTS, model_in)
    stacked = jnp.stack([k_weight, v_weight])
    projected = jnp.einsum(
        "rd,kdc->krc",
        chosen,
        lax.all_gather(stacked, "seq", axis=2, tiled=True),
        preferred_element_type=jnp.float32,
    )
    need_unit, need_inverse = unit_rms(projected[0].reshape(NEED, LATENTS, heads_all, HD))
    keys_need = need_unit.astype(jnp.bfloat16)
    values_need = projected[1].astype(jnp.bfloat16).reshape(NEED, LATENTS, heads_all, HD)
    query_block = queries[0].reshape(tokens_dev, heads_all, HD)
    cot_block = d_context[0].reshape(tokens_dev, heads_all, HD)
    context, d_queries, key_part, value_part = attend(
        query_block, cot_block, local_image, keys_need, values_need
    )
    key_recv_grad, value_recv_grad = (
        lax.all_to_all(
            key_part.reshape(NEED, LATENTS, width), "seq", split_axis=2, concat_axis=0, tiled=True
        ),
        lax.all_to_all(
            value_part.reshape(NEED, LATENTS, width), "seq", split_axis=2, concat_axis=0, tiled=True
        ),
    )
    spread = (needed_slots[None, :] == jnp.arange(image_count, dtype=jnp.int32)[:, None]).astype(
        jnp.bfloat16
    )
    key_cot = jnp.einsum("sr,rlc->slc", spread, key_recv_grad, preferred_element_type=jnp.float32)
    value_cot = jnp.einsum(
        "sr,rlc->slc", spread, value_recv_grad, preferred_element_type=jnp.float32
    )
    key_grad = unit_rms_back(
        key_unit, key_inverse, key_cot.reshape(image_count, LATENTS, heads_dev, HD)
    )
    key_grad = key_grad.astype(jnp.bfloat16).reshape(image_count, LATENTS, cols_dev)
    value_grad = value_cot.astype(jnp.bfloat16)
    grad_k = jnp.einsum(
        "rd,rc->dc",
        flat_slots,
        key_grad.reshape(image_count * LATENTS, cols_dev),
        preferred_element_type=jnp.float32,
    )
    grad_v = jnp.einsum(
        "rd,rc->dc",
        flat_slots,
        value_grad.reshape(image_count * LATENTS, cols_dev),
        preferred_element_type=jnp.float32,
    )
    grad_k, grad_v = (
        lax.psum(grad_k.astype(jnp.bfloat16), "dp").astype(jnp.float32),
        lax.psum(grad_v.astype(jnp.bfloat16), "dp").astype(jnp.float32),
    )
    term = jnp.einsum("ilc,dc->ild", key_grad, k_weight, preferred_element_type=jnp.float32)
    latent_grad = lax.psum_scatter(
        (
            term
            + jnp.einsum("ilc,dc->ild", value_grad, v_weight, preferred_element_type=jnp.float32)
        ).astype(jnp.bfloat16),
        "seq",
        scatter_dimension=0,
        tiled=True,
    )
    return (
        context.reshape(1, tokens_dev, width),
        d_queries.reshape(1, tokens_dev, width),
        latent_grad[None],
        grad_k,
        grad_v,
    )


def solution(mesh):
    in_specs = (
        P("dp", "seq", None),
        P("dp", "seq", None, None),
        P(None, "seq"),
        P(None, "seq"),
        P("dp", "seq", None),
        P("dp", None),
        P("dp", None),
    )
    out_specs = (
        P("dp", "seq", None),
        P("dp", "seq", None),
        P("dp", "seq", None, None),
        P(None, "seq"),
        P(None, "seq"),
    )
    return jax.shard_map(local, mesh=mesh, in_specs=in_specs, out_specs=out_specs, check_vma=False)
```

profile of v0, /device:TPU:1, one launch (start us, length us, event | category | flops | bytes accessed | tf_op | source)
XLA Modules:
  0.0 481.6 jit_solution(536289256523284709)
XLA Ops:
  12.3 5.5 %copy.176 = bf16[64,8,32,128]{3,2,1,0:T(8,128)(2,1)} copy(bf16[64,8,32,128]{3,1,2,0:T(8,128)(2,1)} %bitcast.175) | data formatting | bytes 8388608
  17.8 7.1 %copy.117 = f32[1,512,4096]{1,2,0:T(8,128)} copy(bf16[1,512,4096]{2,1,0:T(8,128)(2,1)} %param.7) | data formatting | bytes 12582912 | tf_op jit(solution)/shard_map/convert_element_type | solution.py:30
  31.2 28.1 %all-gather.6.cloned.1.call-done = bf16[16,1,64,1280]{3,2,1,0:T(8,128)(2,1)} async-done(((bf16[1,1,64,1280]{3,2,1,0:T(8,128)(2,1)}), bf16[16,1,64,1280]{3,2,1,0:T(8,128)(2,1)}) %all-gather.6.cloned.1.call-update) | async-done | bytes 2621456 | tf_op jit(solution)/shard_map/all_gather | solution.py:94
  65.2 137.9 %all-gather.4.cloned.1.call-done = bf16[2,1280,4096]{2,1,0:T(8,128)(2,1)} async-done(((bf16[2,1280,256]{2,1,0:T(8,128)(2,1)}), bf16[2,1280,4096]{2,1,0:T(8,128)(2,1)}) %all-gather.4.cloned.1.call-update) | async-done | bytes 20971536 | tf_op jit(solution)/shard_map/all_gather | solution.py:105
  203.1 9.3 %convolution_bitcast_fusion = f32[2,192,4096]{2,1,0:T(8,128)S(1)} fusion(bf16[192,1280,1]{1,0,2:T(8,128)(2,1)S(1)} %bitcast.180, bf16[2,1280,4096]{2,1,0:T(8,128)(2,1)} %all-gather.4.cloned.1.call-done), kind=kOutput, calls=%fused_computation.19 | convolution fusion | flops 4026531840 | bytes 27754496 | tf_op jit(solution)/shard_map/rd,kdc->krc/dot_general | solution.py:102
  223.4 7.7 %fusion.1 = f32[512,32,64]{0,2,1:T(8,128)} fusion(f32[512,3]{0,1:T(4,128)S(1)} %get-tuple-element.32, bf16[512,32,128,1]{2,1,0,3:T(8,128)(2,1)S(1)} %bitcast.176, bf16[3,64,32,128]{3,2,1,0:T(8,128)(2,1)S(1)} %bitcast.181), kind=kOutput, calls=%fused_computation.4 | convolution fusion | flops 810549248 | bytes 9967616 | tf_op jit(solution)/shard_map/thd,jlhd->thjl/dot_general | solution.py:48
  231.1 6.5 %multiply_convert_fusion.1 = bf16[512,32,64]{0,2,1:T(8,128)(2,1)} fusion(f32[512,32,64]{0,2,1:T(8,128)} %fusion.1, f32[512,32]{0,1:T(8,128)S(1)} %fusion.13, f32[512,32,64]{0,2,1:T(8,128)S(1)} %fusion.2), kind=kOutput, calls=%fused_computation.22 | output fusion | flops 9453631 | bytes 10551296 | tf_op jit(solution)/shard_map/sub | solution.py:53
  237.6 5.3 %fusion.47 = bf16[3,64,32,128]{3,1,0,2:T(8,128)(2,1)S(1)} fusion(bf16[512,32,128,1]{2,1,0,3:T(8,128)(2,1)S(1)} %bitcast.177, bf16[512,3]{0,1:T(4,128)(2,1)S(1)} %get-tuple-element.33, bf16[512,32,64]{0,2,1:T(8,128)(2,1)S(1)} %fusion.77), kind=kOutput, calls=%fused_computation.57 | convolution fusion | flops 809238528 | bytes 7867392 | tf_op jit(solution)/shard_map/thjl,thd->jlhd/dot_general | solution.py:64
  242.9 5.8 %copy.168 = bf16[3,64,32,128]{1,0,3,2:T(4,128)(2,1)} copy(bf16[3,64,32,128]{3,1,0,2:T(8,128)(2,1)S(1)} %fusion.47) | data formatting | bytes 3145728 | tf_op jit(solution)/shard_map/reshape | solution.py:121
  248.7 7.2 %reshape.242 = bf16[16,2,24576]{2,1,0:T(2,128)(2,1)} reshape(bf16[4096,3,64]{2,1,0:T(4,128)(2,1)} %bitcast.166) | data formatting | bytes 3145728
  262.6 5.2 %fusion.46 = f32[32,128,192]{1,2,0:S(1)} fusion(bf16[32,512,192]{1,2,0:T(8,128)(2,1)S(1)} %bitcast.164, f32[512,32,128]{0,2,1:T(8,128)} %bitcast.156, f32[512,32]{0,1:T(8,128)S(1)} %add_rsqrt_fusion.1), kind=kOutput, calls=%fused_computation.56 | convolution fusion | flops 809500672 | bytes 17891328
  269.3 6.4 %copy.161 = bf16[3,64,32,128]{1,0,3,2:T(4,128)(2,1)} copy(bf16[3,64,32,128]{3,1,0,2:T(8,128)(2,1)} %convert_bitcast_fusion) | data formatting | bytes 3145728 | tf_op jit(solution)/shard_map/reshape | solution.py:118
  275.7 7.3 %reshape.240 = bf16[16,2,24576]{2,1,0:T(2,128)(2,1)} reshape(bf16[4096,3,64]{2,1,0:T(4,128)(2,1)} %bitcast.167) | data formatting | bytes 3145728
  282.9 6.7 %all-to-all-start = ((bf16[16,2,24576]{2,1,0:T(2,128)(2,1)}), bf16[16,2,24576]{2,1,0:T(2,128)(2,1)}, u32[]{:S(2)}, u32[]{:S(2)}) async-start(bf16[16,2,24576]{2,1,0:T(2,128)(2,1)} %reshape.240), calls=%async_computation | async-start | bytes 3145728 | tf_op jit(solution)/shard_map/all_to_all | solution.py:117
  294.7 5.2 %copy.170 = bf16[3,64,16,256]{3,1,0,2:T(8,128)(2,1)S(1)} copy(bf16[3,64,16,256]{1,0,3,2:T(4,128)(2,1)} %bitcast.168) | data formatting | bytes 3145728 | tf_op jit(solution)/shard_map/all_to_all | solution.py:120
  309.9 7.1 %reshape.241 = bf16[4096,3,64]{2,1,0:T(4,128)(2,1)} reshape(bf16[16,2,24576]{2,1,0:T(2,128)(2,1)} %all-to-all-done) | data formatting | bytes 3145728
  317.0 6.5 %copy.163 = bf16[3,64,16,256]{3,1,0,2:T(8,128)(2,1)} copy(bf16[3,64,16,256]{1,0,3,2:T(4,128)(2,1)} %bitcast.169) | data formatting | bytes 3145728 | tf_op jit(solution)/shard_map/all_to_all | solution.py:117
  336.3 5.8 %bitcast_convert_fusion = bf16[32,128,512]{2,1,0:T(8,128)(2,1)} fusion(bf16[512,3]{0,1:T(4,128)(2,1)S(1)} %get-tuple-element.33, bf16[512,32,64]{0,2,1:T(8,128)(2,1)} %copy-done.7, bf16[3,64,32,128]{3,2,1,0:T(8,128)(2,1)} %bitcast.182), kind=kOutput, calls=%fused_computation.16 | convolution fusion | flops 810549248 | bytes 7867392 | tf_op jit(solution)/shard_map/thjl,jlhd->thd/dot_general | solution.py:44
  342.1 6.6 %copy.144 = bf16[1,512,4096]{2,1,0:T(8,128)(2,1)} copy(bf16[1,512,4096]{1,2,0:T(8,128)(2,1)} %bitcast.178) | data formatting | bytes 8388608
  348.7 7.6 %fusion.7 = (f32[512,32]{0,1:T(8,128)S(1)}, f32[32,128,512,1]{2,1,3,0:T(8,128)}) fusion(f32[512,32,128]{0,2,1:T(8,128)} %bitcast.157, f32[512,32]{0,1:T(8,128)S(1)} %add_rsqrt_fusion.1, bf16[512,32,64]{0,2,1:T(8,128)(2,1)} %multiply_convert_fusion.1, bf16[512,3]{0,1:T(4,128)(2,1)S(1)} %get-tuple-element.33, bf16[3,64,32,128]{3,2,1,0:T(8,128)(2,1)S(1)} %fusion.19), kind=kOutput, calls=%fused_computation.13 | convolution fusion | flops 814727168 | bytes 20581376 | tf_op jit(solution)/shard_map/thjl,jlhd->thd/dot_general | solution.py:57
  356.3 10.9 %fusion.9 = bf16[512,32,128]{0,2,1:T(8,128)(2,1)} fusion(f32[32,128,512,1]{2,1,3,0:T(8,128)} %get-tuple-element.35, f32[512,32,128]{0,2,1:T(8,128)} %bitcast.158, f32[512,32]{0,1:T(8,128)S(1)} %broadcast_multiply_fusion.1, f32[512,32]{0,1:T(8,128)S(1)} %add_rsqrt_fusion.1), kind=kLoop, calls=%fused_computation.15 | loop fusion | flops 10485760 | bytes 21102592 | tf_op jit(solution)/shard_map/convert_element_type | solution.py:60
  367.2 6.3 %copy.145 = bf16[1,512,4096]{2,1,0:T(8,128)(2,1)} copy(bf16[1,512,4096]{1,2,0:T(8,128)(2,1)} %bitcast.165) | data formatting | bytes 8388608
  373.6 22.5 %all-reduce.4.cloned.1.call-done = (bf16[1280,256]{0,1:T(8,128)(2,1)}, bf16[1280,256]{0,1:T(8,128)(2,1)}) async-done(((bf16[1280,256]{0,1:T(8,128)(2,1)}, bf16[1280,256]{0,1:T(8,128)(2,1)}), (bf16[1280,256]{0,1:T(8,128)(2,1)}, bf16[1280,256]{0,1:T(8,128)(2,1)})) %all-reduce.4.cloned.1.call-update) | async-done | bytes 1310736 | tf_op jit(solution)/shard_map/psum | solution.py:149
  400.9 73.7 %reduce-scatter.4.cloned.1.call-done = bf16[1,64,1280]{2,1,0:T(8,128)(2,1)} async-done(((bf16[16,64,1280]{2,1,0:T(8,128)(2,1)}), bf16[1,64,1280]{2,1,0:T(8,128)(2,1)}) %reduce-scatter.4.cloned.1.call-update) | async-done | bytes 163856
  (90 shorter events, 68.8 us)
Async XLA Ops:
  7.2 17.7 %copy-start = (s32[1,16]{1,0:T(1,128)S(1)}, s32[1,16]{1,0:T(1,128)}, u32[]{:S(2)}) copy-start(s32[1,16]{1,0:T(1,128)} %param.13) | copy-start | bytes 196
  7.2 4.9 %copy-start.2 = (bf16[1280,256]{1,0:T(8,128)(2,1)S(1)}, bf16[1280,256]{1,0:T(8,128)(2,1)}, u32[]{:S(2)}) copy-start(bf16[1280,256]{1,0:T(8,128)(2,1)} %param.9) | copy-start | bytes 1966084
  7.2 52.1 %all-gather.6.cloned.1.call-start = ((), (), s32[]{:S(2)}) async-start(), calls=%async_computation.4 | async-start | bytes 2785280 | tf_op jit(solution)/shard_map/all_gather | solution.py:94
  7.9 195.1 %all-gather.4.cloned.1.call-start = ((), (), s32[]{:S(2)}) async-start(), calls=%async_computation.3 | async-start | bytes 22282240 | tf_op jit(solution)/shard_map/all_gather | solution.py:105
  24.9 0.9 copy-start.12
  212.9 3.0 slice-start
  213.4 3.6 slice-start.1
  213.8 7.6 %copy-start.10 = (bf16[24,8,32,128]{3,2,1,0:T(8,128)(2,1)}, bf16[24,8,32,128]{3,2,1,0:T(8,128)(2,1)S(1)}, u32[]{:S(2)}) copy-start(bf16[24,8,32,128]{3,2,1,0:T(8,128)(2,1)S(1)} %copy.174) | copy-start | bytes 4718596
  220.5 2.9 copy-start.4
  221.4 16.2 %copy-start.7 = (bf16[512,32,64]{0,2,1:T(8,128)(2,1)}, bf16[512,32,64]{0,2,1:T(8,128)(2,1)S(1)}, u32[]{:S(2)}) copy-start(bf16[512,32,64]{0,2,1:T(8,128)(2,1)S(1)} %fusion.77) | copy-start | bytes 6291460
  255.9 27.0 %all-to-all-start.1 = ((bf16[16,2,24576]{2,1,0:T(2,128)(2,1)}), bf16[16,2,24576]{2,1,0:T(2,128)(2,1)S(1)}, u32[]{:S(2)}, u32[]{:S(2)}) async-start(bf16[16,2,24576]{2,1,0:T(2,128)(2,1)} %reshape.242), calls=%async_computation.1 | async-start | bytes 3145728 | tf_op jit(solution)/shard_map/all_to_all | solution.py:120
  282.9 26.9 %all-to-all-start = ((bf16[16,2,24576]{2,1,0:T(2,128)(2,1)}), bf16[16,2,24576]{2,1,0:T(2,128)(2,1)}, u32[]{:S(2)}, u32[]{:S(2)}) async-start(bf16[16,2,24576]{2,1,0:T(2,128)(2,1)} %reshape.240), calls=%async_computation | async-start | bytes 3145728 | tf_op jit(solution)/shard_map/all_to_all | solution.py:117
  289.7 106.4 %all-reduce.4.cloned.1.call-start = ((), (), s32[]{:S(2)}) async-start(), calls=%async_computation.6 | async-start | bytes 2621440 | tf_op jit(solution)/shard_map/psum | solution.py:149
  300.9 0.8 copy-start.8
  325.9 3.3 copy-start.5
  325.9 5.0 %copy-start.11 = (bf16[16,1,64,1280]{3,2,1,0:T(8,128)(2,1)S(1)}, bf16[16,1,64,1280]{3,2,1,0:T(8,128)(2,1)}, u32[]{:S(2)}) copy-start(bf16[16,1,64,1280]{3,2,1,0:T(8,128)(2,1)} %all-gather.6.cloned.1.call-done) | copy-start | bytes 7864324
  329.2 3.5 copy-start.3
  332.6 1.1 copy-start.6
  332.6 142.0 %reduce-scatter.4.cloned.1.call-start = ((), (), s32[]{:S(2)}) async-start(), calls=%async_computation.5 | async-start | bytes 2785280
  332.7 1.2 copy-start.9
  367.2 107.3 %copy-start.1 = (s32[1,16]{1,0:T(1,128)S(1)}, s32[1,16]{1,0:T(1,128)}, u32[]{:S(2)}) copy-start(s32[1,16]{1,0:T(1,128)} %param.13) | copy-start | bytes 196
Sparse Core Ops, SparseCore 0:
  10.2 48.9 all-gather.5
  61.9 141.0 all-gather.3
  332.7 63.3 all-reduce.3
  399.8 74.6 reduce-scatter.3
where the time goes:
time: 491 us; the launch traced here: 482 us
  waiting for transfers between devices  267 us (54%)
  local copies, waits for them, and re-layouts  93.4 us (19%)
  matrix products  58.5 us (12%)
  other arithmetic  36.9 us (8%)
  between operations  14.7 us (3%)
  starting transfers between devices  11.5 us (2%)
    all_gather x1, waiting for transfers between devices, local(): lax.all_gather(stacked, 'seq', axis=2, tiled=True)  138 us
    unnamed x5, waiting for transfers between devices  74.5 us
    unnamed x43, local copies, waits for them, and re-layouts  55.5 us
    all_gather x1, waiting for transfers between devices, local(): gathered = lax.all_gather(latents[0], 'seq', axis=0, tiled=True)  28.1 us
    psum x1, waiting for transfers between devices, local(): lax.psum(grad_k.astype(jnp.bfloat16), 'dp').astype(jnp.float32)  22.5 us
    convert_element_type x1, other arithmetic, attend(): unit_rms_back(query_unit, query_inverse, query_cot).astype(jnp.bfloat16)  10.9 us
  transfers between devices with their start and end apart: 6, of which 5 were waited for; matrix products, arithmetic and copies ran while one was open for 23% of the time, Pallas kernels for 0%

commit v1 on v0

v1 whole, which is shorter than its diff:
```python
import math

import jax
import jax.numpy as jnp
from jax import lax
from jax.experimental import pallas as pl
from jax.experimental.pallas import tpu as pltpu
from jax.sharding import PartitionSpec as P

HD = 128
LATENTS = 64
NEED = 3
SIDE = 4
SEQ = 16
ROWS = NEED * LATENTS
EPSILON = 1e-06
SCALE = 1.0 / math.sqrt(HD)
MESH = pl.DeviceIdType.MESH
F32 = jnp.float32
BF16 = jnp.bfloat16

OFFSETS = (
    (0, 0),
    (1, 0),
    (3, 0),
    (0, 1),
    (0, 3),
    (2, 0),
    (0, 2),
    (1, 1),
    (3, 3),
    (1, 3),
    (3, 1),
    (2, 1),
    (1, 2),
    (2, 3),
    (3, 2),
    (2, 2),
)
X_CODE = sum(o[0] << (2 * i) for i, o in enumerate(OFFSETS[1:]))
Y_CODE = sum(o[1] << (2 * i) for i, o in enumerate(OFFSETS[1:]))


def offset_of(step):
    place = 2 * lax.rem(step + SEQ - 1, SEQ)
    return (
        lax.rem(lax.shift_right_logical(jnp.int32(X_CODE), place), SIDE),
        lax.rem(lax.shift_right_logical(jnp.int32(Y_CODE), place), SIDE),
    )


def nt(a, b):
    return lax.dot_general(a, b, (((1,), (1,)), ((), ())), preferred_element_type=F32)


def tn(a, b):
    return lax.dot_general(a, b, (((0,), (0,)), ((), ())), preferred_element_type=F32)


def nn(a, b):
    return lax.dot_general(a, b, (((1,), (0,)), ((), ())), preferred_element_type=F32)


def mean_last(a):
    return jnp.mean(a, axis=-1, keepdims=True)


def attend_half(query, cotangent, keys, values, image):
    raw = query.astype(F32)
    inverse = lax.rsqrt(mean_last(raw * raw) + EPSILON)
    unit = raw * inverse
    unit_b = unit.astype(BF16)
    is0, is1, is2 = image == 0, image == 1, image == 2

    def choose(wide):
        return jnp.where(
            is0, wide[:LATENTS], jnp.where(is1, wide[LATENTS : 2 * LATENTS], wide[2 * LATENTS :])
        )

    def widen(narrow):
        return jnp.concatenate(
            [jnp.where(own, narrow, 0.0).astype(BF16) for own in (is0, is1, is2)], axis=0
        )

    exponent = jnp.exp(choose(nt(keys, unit_b)) * SCALE)
    probs = exponent * (1.0 / jnp.sum(exponent, axis=0, keepdims=True))
    dprob = choose(nt(values, cotangent))
    dscore = probs * (dprob - jnp.sum(probs * dprob, axis=0, keepdims=True)) * SCALE
    probs_wide = widen(probs)
    dscore_wide = widen(dscore)
    context = tn(probs_wide, values)
    query_cot = tn(dscore_wide, keys)
    d_query = inverse * (query_cot - unit * mean_last(query_cot * unit))
    return (
        context.astype(BF16),
        d_query.astype(BF16),
        nn(dscore_wide, unit_b),
        nn(probs_wide, cotangent),
    )


def attention_kernel(
    pos_ref, slot_ref, lat_ref, kw_ref, vw_ref, q_hbm, c_hbm,
    ctx_hbm, dq_hbm, grad_ref, lat_out,
    lat_all, raw_ref, kv_ref, kv_send, kv_recv, g_send, g_recv, run_ref, img_ref,
    q_buf, c_buf, ctx_buf, dq_buf, first_ref, last_ref,
    a_send, a_recv, f_send, f_recv, b_send, b_recv, q_sem, c_sem, ctx_sem, dq_sem, lat_sem,
):
    tokens = q_hbm.shape[0]
    cols = kw_ref.shape[1]
    wide = 2 * cols
    dp = lax.axis_index("dp")
    me = lax.axis_index("seq")
    mx = lax.div(me, SIDE)
    my = lax.rem(me, SIDE)

    def peer(dx, dy):
        return (dp, lax.rem(mx + dx + SIDE, SIDE) * SIDE + lax.rem(my + dy + SIDE, SIDE))

    def owner_of(step):
        dx, dy = offset_of(step)
        return lax.rem(mx - dx + SIDE, SIDE) * SIDE + lax.rem(my - dy + SIDE, SIDE)

    def part(ref, owner):
        return ref.at[:, pl.ds(pl.multiple_of(owner * cols, cols), cols)]

    def q_copy(step):
        return pltpu.make_async_copy(part(q_hbm, owner_of(step)), q_buf.at[step], q_sem.at[step])

    def c_copy(step):
        return pltpu.make_async_copy(part(c_hbm, owner_of(step)), c_buf.at[step], c_sem.at[step])

    def ctx_copy(step):
        return pltpu.make_async_copy(
            ctx_buf.at[step], part(ctx_hbm, owner_of(step)), ctx_sem.at[step]
        )

    def dq_copy(step):
        return pltpu.make_async_copy(dq_buf.at[step], part(dq_hbm, owner_of(step)), dq_sem.at[step])

    barrier = pltpu.get_barrier_semaphore()
    for dx, dy in OFFSETS[1:]:
        pl.semaphore_signal(barrier, inc=1, device_id=peer(dx, dy), device_id_type=MESH)

    half = LATENTS // 2
    lat_all[mx, my] = lat_ref[...]

    def x_first(d):
        src = lat_ref.at[pl.ds(0, half)]
        return pltpu.make_async_remote_copy(
            src_ref=src,
            dst_ref=lat_all.at[mx, my, pl.ds(0, half)],
            send_sem=a_send.at[0, d - 1],
            recv_sem=a_recv.at[0, d - 1],
            device_id=peer(d, 0),
            device_id_type=MESH,
        )

    def y_first(d):
        src = lat_ref.at[pl.ds(half, half)]
        return pltpu.make_async_remote_copy(
            src_ref=src,
            dst_ref=lat_all.at[mx, my, pl.ds(half, half)],
            send_sem=a_send.at[1, d - 1],
            recv_sem=a_recv.at[1, d - 1],
            device_id=peer(0, d),
            device_id_type=MESH,
        )

    def y_second(d):
        block = lat_all.at[:, my, pl.ds(0, half)]
        return pltpu.make_async_remote_copy(
            src_ref=block,
            dst_ref=block,
            send_sem=a_send.at[2, d - 1],
            recv_sem=a_recv.at[2, d - 1],
            device_id=peer(0, d),
            device_id_type=MESH,
        )

    def x_second(d):
        block = lat_all.at[mx, :, pl.ds(half, half)]
        return pltpu.make_async_remote_copy(
            src_ref=block,
            dst_ref=block,
            send_sem=a_send.at[3, d - 1],
            recv_sem=a_recv.at[3, d - 1],
            device_id=peer(d, 0),
            device_id_type=MESH,
        )

    pl.semaphore_wait(barrier, SEQ - 1)
    for d in (1, 3, 2):
        x_first(d).start()
        y_first(d).start()

    def fetch(step, carry):
        q_copy(step).start()
        c_copy(step).start()
        return carry

    lax.fori_loop(0, SEQ, fetch, 0)

    def block_images(block, carry):
        count = jnp.int32(-1)
        for i in range(SEQ):
            count = count + (pos_ref[0, i] <= block * tokens).astype(jnp.int32)
        first_ref[block] = count
        return carry

    lax.fori_loop(0, SEQ, block_images, 0)

    def slot_last(slot, carry):
        image = jnp.int32(0)
        for i in range(SEQ):
            image = image + jnp.where(slot_ref[0, i] == slot, i, 0)
        image = jnp.minimum(image, SEQ - 1)
        after = pos_ref[0, jnp.minimum(image + 1, SEQ - 1)]
        end = jnp.where(image == SEQ - 1, SEQ * tokens, after) - 1
        block = jnp.maximum(lax.div(end, tokens), 0)
        place = jnp.clip(image - first_ref[block], 0, NEED - 1)
        last_ref[slot] = block * NEED + place
        return carry

    lax.fori_loop(0, SEQ, slot_last, 0)

    token = me * tokens + lax.broadcasted_iota(jnp.int32, (1, tokens), 1)
    seen = jnp.zeros((1, tokens), jnp.int32) - 1 - first_ref[me]
    for i in range(SEQ):
        seen = seen + (token >= pos_ref[0, i]).astype(jnp.int32)
    img_ref[...] = seen

    for d in (1, 3, 2):
        x_first(d).wait_recv()
    for d in (1, 3, 2):
        y_second(d).start()
    for d in (1, 3, 2):
        y_first(d).wait_recv()
    for d in (1, 3, 2):
        x_second(d).start()
    for d in (1, 3, 2):
        y_second(d).wait_recv()
        x_second(d).wait_recv()
    lat_copy = pltpu.make_async_copy(lat_all, lat_out, lat_sem)
    lat_copy.start()

    def project(chunk, carry):
        rows = pl.ds(pl.multiple_of(chunk * SIDE * LATENTS, SIDE * LATENTS), SIDE * LATENTS)
        slots = pl.ds(chunk * SIDE, SIDE)
        latents = lat_all[chunk].reshape(SIDE * LATENTS, lat_ref.shape[1])
        raw = nn(latents, kw_ref[...])
        raw_ref[rows, :] = raw
        for head in range(cols // HD):
            one = raw[:, head * HD : (head + 1) * HD]
            unit = one * lax.rsqrt(mean_last(one * one) + EPSILON)
            kv_ref[slots, :, head * HD : (head + 1) * HD] = unit.astype(BF16).reshape(
                SIDE, LATENTS, HD
            )
        values = nn(latents, vw_ref[...]).astype(BF16)
        kv_ref[slots, :, cols:] = values.reshape(SIDE, LATENTS, cols)
        return carry

    lax.fori_loop(0, SIDE, project, 0)

    def forward(step):
        dx, dy = offset_of(step)
        return pltpu.make_async_remote_copy(
            src_ref=kv_send.at[step],
            dst_ref=kv_recv.at[step],
            send_sem=f_send.at[step],
            recv_sem=f_recv.at[step],
            device_id=peer(dx, dy),
            device_id_type=MESH,
        )

    def backward(step):
        return pltpu.make_async_remote_copy(
            src_ref=g_send.at[step],
            dst_ref=g_recv.at[me],
            send_sem=b_send.at[step],
            recv_sem=b_recv.at[me],
            device_id=(dp, owner_of(step)),
            device_id_type=MESH,
        )

    def arrival(block):
        return pltpu.make_async_remote_copy(
            src_ref=g_send.at[0],
            dst_ref=g_recv.at[block],
            send_sem=b_send.at[0],
            recv_sem=b_recv.at[block],
            device_id=(dp, block),
            device_id_type=MESH,
        )

    def needed(block, j):
        slot = slot_ref[0, jnp.minimum(first_ref[block] + j, SEQ - 1)]
        return kv_ref[slot]

    for j in range(NEED):
        kv_recv[0, j * LATENTS : (j + 1) * LATENTS, :] = needed(me, j)

    def send(step, carry):
        dx, dy = offset_of(step)
        block = peer(dx, dy)[1]
        for j in range(NEED):
            kv_send[step, j * LATENTS : (j + 1) * LATENTS, :] = needed(block, j)
        forward(step).start()
        return carry

    lax.fori_loop(1, SEQ, send, 0)

    def attend(step, carry):
        @pl.when(step > 0)
        def _():
            forward(step).wait_recv()

        q_copy(step).wait()
        c_copy(step).wait()
        for head in range(cols // HD):
            lanes = slice(head * HD, (head + 1) * HD)
            lanes_v = slice(cols + head * HD, cols + (head + 1) * HD)
            keys = kv_recv[step, :, lanes]
            values = kv_recv[step, :, lanes_v]
            key_part = jnp.zeros((ROWS, HD), F32)
            value_part = jnp.zeros((ROWS, HD), F32)
            size = 256
            for begin in range(0, tokens, size):
                rows = slice(begin, begin + size)
                context, d_query, key_add, value_add = attend_half(
                    q_buf[step, rows, lanes],
                    c_buf[step, rows, lanes],
                    keys,
                    values,
                    img_ref[:, rows],
                )
                ctx_buf[step, rows, lanes] = context
                dq_buf[step, rows, lanes] = d_query
                key_part = key_part + key_add
                value_part = value_part + value_add
            g_send[step, :, lanes] = key_part.astype(BF16)
            g_send[step, :, lanes_v] = value_part.astype(BF16)

        ctx_copy(step).start()
        dq_copy(step).start()

        @pl.when(step > 0)
        def _():
            backward(step).start()

        @pl.when(step == 0)
        def _():
            g_recv[me] = g_send[0]

        return carry

    lax.fori_loop(0, SEQ, attend, 0)

    def combine(block, run):
        @pl.when(block != me)
        def _():
            arrival(block).wait_recv()

        first = first_ref[block]
        end = (block + 1) * tokens - 1
        before = block * tokens - 1
        last = jnp.int32(-1)
        previous = jnp.int32(-1)
        for i in range(SEQ):
            last = last + (pos_ref[0, i] <= end).astype(jnp.int32)
            previous = previous + (pos_ref[0, i] <= before).astype(jnp.int32)
        for j in range(NEED):
            same = previous == first if j == 0 else first + j > last
            keep = jnp.where(same, 1.0, 0.0).astype(F32)
            run = run * keep + g_recv[block, j * LATENTS : (j + 1) * LATENTS, :].astype(F32)
            run_ref[block * NEED + j] = run
        return run

    lax.fori_loop(0, SEQ, combine, jnp.zeros((LATENTS, wide), F32))

    def key_grads(slot, carry):
        rows = pl.ds(pl.multiple_of(slot * LATENTS, LATENTS), LATENTS)
        total = run_ref[last_ref[slot]]
        for head in range(cols // HD):
            lanes = slice(head * HD, (head + 1) * HD)
            raw = raw_ref[rows, lanes]
            cot = total[:, lanes]
            inverse = lax.rsqrt(mean_last(raw * raw) + EPSILON)
            unit = raw * inverse
            grad_ref[rows, lanes] = (inverse * (cot - unit * mean_last(cot * unit))).astype(BF16)
        grad_ref[rows, cols:] = total[:, cols:].astype(BF16)
        return carry

    lax.fori_loop(0, SEQ, key_grads, 0)

    for d in (1, 2, 3):
        x_first(d).wait_send()
        y_first(d).wait_send()
        y_second(d).wait_send()
        x_second(d).wait_send()
    lat_copy.wait()

    def drain(step, carry):
        @pl.when(step > 0)
        def _():
            forward(step).wait_send()
            backward(step).wait_send()

        ctx_copy(step).wait()
        dq_copy(step).wait()
        return carry

    lax.fori_loop(0, SEQ, drain, 0)


def attention_call(positions, slots, latents, k_weight, v_weight, queries, cotangents):
    tokens, width = queries.shape
    cols = k_weight.shape[1]
    model = latents.shape[1]
    wide = 2 * cols
    smem = pl.BlockSpec(memory_space=pltpu.SMEM)
    vmem = pl.BlockSpec(memory_space=pltpu.VMEM)
    hbm = pl.BlockSpec(memory_space=pl.ANY)
    dma = pltpu.SemaphoreType.DMA
    return pl.pallas_call(
        attention_kernel,
        name="attention",
        out_shape=(
            jax.ShapeDtypeStruct((tokens, width), BF16),
            jax.ShapeDtypeStruct((tokens, width), BF16),
            jax.ShapeDtypeStruct((SEQ * LATENTS, wide), BF16),
            jax.ShapeDtypeStruct((SIDE, SIDE, LATENTS, model), BF16),
        ),
        in_specs=[smem, smem, vmem, vmem, vmem, hbm, hbm],
        out_specs=(hbm, hbm, vmem, hbm),
        scratch_shapes=[
            pltpu.VMEM((SIDE, SIDE, LATENTS, model), BF16),
            pltpu.VMEM((SEQ * LATENTS, cols), F32),
            pltpu.VMEM((SEQ, LATENTS, wide), BF16),
            pltpu.VMEM((SEQ, ROWS, wide), BF16),
            pltpu.VMEM((SEQ, ROWS, wide), BF16),
            pltpu.VMEM((SEQ, ROWS, wide), BF16),
            pltpu.VMEM((SEQ, ROWS, wide), BF16),
            pltpu.VMEM((SEQ * NEED, LATENTS, wide), F32),
            pltpu.VMEM((1, tokens), jnp.int32),
            pltpu.VMEM((SEQ, tokens, cols), BF16),
            pltpu.VMEM((SEQ, tokens, cols), BF16),
            pltpu.VMEM((SEQ, tokens, cols), BF16),
            pltpu.VMEM((SEQ, tokens, cols), BF16),
            pltpu.SMEM((SEQ,), jnp.int32),
            pltpu.SMEM((SEQ,), jnp.int32),
            dma((4, SIDE - 1)),
            dma((4, SIDE - 1)),
            dma((SEQ,)),
            dma((SEQ,)),
            dma((SEQ,)),
            dma((SEQ,)),
            dma((SEQ,)),
            dma((SEQ,)),
            dma((SEQ,)),
            dma((SEQ,)),
            dma(()),
        ],
        compiler_params=pltpu.CompilerParams(
            collective_id=0, has_side_effects=True, vmem_limit_bytes=56 * 2**20
        ),
    )(positions, slots, latents, k_weight, v_weight, queries, cotangents)


def gradient_kernel(
    grad_ref, lat_ref, kw_ref, vw_ref,
    dlat_ref, dw_ref,
    dw_send, core_recv, z_send, z_recv, final_ref, da_send, db_send, da_recv, db_recv, ea_send, eb_send, ea_recv, eb_recv,
    core_ss, core_rs, z_ss, z_rs, g_ss, g_rs, h_ss, h_rs, a_ss, a_rs, b_ss, b_rs, ea_ss, ea_rs, eb_ss, eb_rs,
):
    model = kw_ref.shape[0]
    cols = kw_ref.shape[1]
    half = model // 2
    piece = half // SIDE
    dp = lax.axis_index("dp")
    me = lax.axis_index("seq")
    mx = lax.div(me, SIDE)
    my = lax.rem(me, SIDE)
    mz = lax.div(dp, 2)
    core = lax.rem(dp, 2)

    def ring(base, d):
        return lax.rem(base + d, SIDE)

    def x_peer(d):
        return (dp, ring(mx, d) * SIDE + my)

    def y_peer(d):
        return (dp, mx * SIDE + ring(my, d))

    def z_peer(d):
        return (ring(mz, d) * 2 + core, me)

    core_peer = (mz * 2 + 1 - core, me)

    def remote(src, dst, send_sem, recv_sem, device):
        return pltpu.make_async_remote_copy(
            src_ref=src,
            dst_ref=dst,
            send_sem=send_sem,
            recv_sem=recv_sem,
            device_id=device,
            device_id_type=MESH,
        )

    barrier = pltpu.get_barrier_semaphore()
    for d in (1, 2, 3):
        for device in (x_peer(d), y_peer(d), z_peer(d)):
            pl.semaphore_signal(barrier, inc=1, device_id=device, device_id_type=MESH)
    pl.semaphore_signal(barrier, inc=1, device_id=core_peer, device_id_type=MESH)

    chunk = 128

    def weight_grad(base):
        def one(i, carry):
            rows = pl.ds(pl.multiple_of(base + i * chunk, chunk), chunk)
            dw_send[rows, :] = tn(lat_ref[:, rows], grad_ref[...]).astype(BF16)
            return carry

        lax.fori_loop(0, half // chunk, one, 0)

    own_rows = pl.multiple_of(core * half, half)
    other_rows = pl.multiple_of((1 - core) * half, half)
    core_copy = remote(
        dw_send.at[pl.ds(other_rows, half)], core_recv, core_ss, core_rs, core_peer
    )

    def da_copy(d):
        return remote(
            da_send.at[ring(mx, d)], da_recv.at[d - 1], a_ss.at[d - 1], a_rs.at[d - 1], x_peer(d)
        )

    def db_copy(d):
        return remote(
            db_send.at[:, ring(my, d)], db_recv.at[d - 1], b_ss.at[d - 1], b_rs.at[d - 1], y_peer(d)
        )

    def ea_copy(d):
        return remote(
            ea_send.at[ring(my, d)], ea_recv.at[d - 1], ea_ss.at[d - 1], ea_rs.at[d - 1], y_peer(d)
        )

    def eb_copy(d):
        return remote(
            eb_send.at[ring(mx, d)], eb_recv.at[d - 1], eb_ss.at[d - 1], eb_rs.at[d - 1], x_peer(d)
        )

    def z_copy(d):
        rows = pl.ds(pl.multiple_of(ring(mz, d) * piece, 32), piece)
        return remote(z_send.at[rows], z_recv.at[d - 1], z_ss.at[d - 1], z_rs.at[d - 1], z_peer(d))

    def final_rows(z, c):
        return pl.ds(pl.multiple_of(c * half + z * piece, 32), piece)

    def g_copy(d):
        block = final_ref.at[final_rows(mz, core)]
        return remote(block, block, g_ss.at[d - 1], g_rs.at[d - 1], z_peer(d))

    def h_copy(d):
        block = final_ref.at[final_rows(ring(mz, SIDE - d), core)]
        return remote(block, block, h_ss.at[d], h_rs.at[d], core_peer)

    weight_grad(other_rows)
    pl.semaphore_wait(barrier, 3 * (SIDE - 1) + 1)
    core_copy.start()

    def latent_grad(x):
        rows = pl.ds(pl.multiple_of(x * SIDE * LATENTS, SIDE * LATENTS), SIDE * LATENTS)
        keys = grad_ref[rows, :cols]
        values = grad_ref[rows, cols:]
        shape = (SIDE, LATENTS, half)
        da_send[x] = (
            (nt(keys, kw_ref[:half]) + nt(values, vw_ref[:half])).astype(BF16).reshape(shape)
        )
        db_send[x] = (
            (nt(keys, kw_ref[half:]) + nt(values, vw_ref[half:])).astype(BF16).reshape(shape)
        )

    def latent_grads(d, carry):
        latent_grad(ring(mx, d))

        @pl.when(d > 0)
        def _():
            da_copy(d).start()

        return carry

    lax.fori_loop(0, SIDE, latent_grads, 0)
    for d in (1, 3, 2):
        db_copy(d).start()

    weight_grad(own_rows)
    core_copy.wait_recv()

    def core_sum(i, carry):
        rows = pl.ds(pl.multiple_of(i * piece, 32), piece)
        own = pl.ds(pl.multiple_of(own_rows + i * piece, 32), piece)
        z_send[rows, :] = (dw_send[own, :].astype(F32) + core_recv[rows, :].astype(F32)).astype(
            BF16
        )
        return carry

    lax.fori_loop(0, SIDE, core_sum, 0)
    for d in (1, 3, 2):
        z_copy(d).start()

    for d in (1, 2, 3):
        da_copy(d).wait_recv()

    def sum_a(y, carry):
        total = da_send[mx, y].astype(F32)
        for d in range(SIDE - 1):
            total = total + da_recv[d, y].astype(F32)
        ea_send[y] = total.astype(BF16)
        return carry

    lax.fori_loop(0, SIDE, sum_a, 0)
    for d in (1, 3, 2):
        ea_copy(d).start()
    for d in (1, 2, 3):
        db_copy(d).wait_recv()

    def sum_b(x, carry):
        total = db_send[x, my].astype(F32)
        for d in range(SIDE - 1):
            total = total + db_recv[d, x].astype(F32)
        eb_send[x] = total.astype(BF16)
        return carry

    lax.fori_loop(0, SIDE, sum_b, 0)
    for d in (1, 3, 2):
        eb_copy(d).start()

    for d in (1, 2, 3):
        z_copy(d).wait_recv()
    own_piece = pl.ds(pl.multiple_of(mz * piece, 32), piece)
    total = z_send[own_piece, :].astype(F32)
    for d in range(SIDE - 1):
        total = total + z_recv[d].astype(F32)
    final_ref[final_rows(mz, core), :] = total.astype(BF16)
    for d in (1, 3, 2):
        g_copy(d).start()
    h_copy(0).start()

    for d in (1, 2, 3):
        ea_copy(d).wait_recv()
    total = ea_send[my].astype(F32)
    for d in range(SIDE - 1):
        total = total + ea_recv[d].astype(F32)
    dlat_ref[:, :half] = total.astype(BF16)
    for d in (1, 2, 3):
        eb_copy(d).wait_recv()
    total = eb_send[mx].astype(F32)
    for d in range(SIDE - 1):
        total = total + eb_recv[d].astype(F32)
    dlat_ref[:, half:] = total.astype(BF16)

    for d in (1, 3, 2):
        g_copy(d).wait_recv()
        h_copy(d).start()
    for d in range(SIDE):
        h_copy(d).wait_recv()

    def write(i, carry):
        rows = pl.ds(pl.multiple_of(i * piece, 32), piece)
        dw_ref[rows, :] = final_ref[rows, :]
        return carry

    lax.fori_loop(0, 2 * SIDE, write, 0)

    core_copy.wait_send()
    for d in (1, 2, 3):
        for copy in (da_copy(d), db_copy(d), ea_copy(d), eb_copy(d), z_copy(d), g_copy(d)):
            copy.wait_send()
    for d in range(SIDE):
        h_copy(d).wait_send()


def gradient_call(grads, latents, k_weight, v_weight):
    model, cols = k_weight.shape
    half = model // 2
    piece = half // SIDE
    wide = 2 * cols
    vmem = pl.BlockSpec(memory_space=pltpu.VMEM)
    dma = pltpu.SemaphoreType.DMA
    peers = SIDE - 1
    return pl.pallas_call(
        gradient_kernel,
        name="gradients",
        out_shape=(
            jax.ShapeDtypeStruct((LATENTS, model), BF16),
            jax.ShapeDtypeStruct((model, wide), BF16),
        ),
        in_specs=[vmem] * 4,
        out_specs=(vmem, vmem),
        scratch_shapes=[
            pltpu.VMEM((model, wide), BF16),
            pltpu.VMEM((half, wide), BF16),
            pltpu.VMEM((half, wide), BF16),
            pltpu.VMEM((peers, piece, wide), BF16),
            pltpu.VMEM((model, wide), BF16),
            pltpu.VMEM((SIDE, SIDE, LATENTS, half), BF16),
            pltpu.VMEM((SIDE, SIDE, LATENTS, half), BF16),
            pltpu.VMEM((peers, SIDE, LATENTS, half), BF16),
            pltpu.VMEM((peers, SIDE, LATENTS, half), BF16),
            pltpu.VMEM((SIDE, LATENTS, half), BF16),
            pltpu.VMEM((SIDE, LATENTS, half), BF16),
            pltpu.VMEM((peers, LATENTS, half), BF16),
            pltpu.VMEM((peers, LATENTS, half), BF16),
            dma(()),
            dma(()),
            dma((peers,)),
            dma((peers,)),
            dma((peers,)),
            dma((peers,)),
            dma((SIDE,)),
            dma((SIDE,)),
        ]
        + [dma((peers,))] * 8,
        compiler_params=pltpu.CompilerParams(
            collective_id=1, has_side_effects=True, vmem_limit_bytes=56 * 2**20
        ),
    )(grads, latents, k_weight, v_weight)


def local(queries, latents, k_weight, v_weight, d_context, image_pos, image_slot):
    model, cols = k_weight.shape
    context, d_queries, grads, lat_all = attention_call(
        image_pos, image_slot, latents[0, 0], k_weight, v_weight, queries[0], d_context[0]
    )
    d_latents, d_weights = gradient_call(
        grads, lat_all.reshape(SEQ * LATENTS, model), k_weight, v_weight
    )
    d_weights = d_weights.astype(F32)
    return (
        context[None],
        d_queries[None],
        d_latents[None, None],
        d_weights[:, :cols],
        d_weights[:, cols:],
    )


def solution(mesh):
    in_specs = (
        P("dp", "seq", None),
        P("dp", "seq", None, None),
        P(None, "seq"),
        P(None, "seq"),
        P("dp", "seq", None),
        P("dp", None),
        P("dp", None),
    )
    out_specs = (
        P("dp", "seq", None),
        P("dp", "seq", None),
        P("dp", "seq", None, None),
        P(None, "seq"),
        P(None, "seq"),
    )
    return jax.shard_map(local, mesh=mesh, in_specs=in_specs, out_specs=out_specs, check_vma=False)
```

time: 491 us -> 156 us (0.32); the launches traced: 482 us -> 155 us
  waiting for transfers between devices: 267 us -> 0 us
  Pallas kernels: 0 us -> 145 us
  local copies, waits for them, and re-layouts: 93.4 us -> 9.52 us
  matrix products: 58.5 us -> 0 us
  other arithmetic: 36.9 us -> 0 us
  between operations: 14.7 us -> 0.66 us
  starting transfers between devices: 11.5 us -> 0 us
    all_gather x2 -> x0, waiting for transfers between devices: 166 us -> none  [the longest x1 138 us: local(): lax.all_gather(stacked, 'seq', axis=2, tiled=True)]
    pallas_call x0 -> x2, Pallas kernels: none -> 145 us  [the longest x1 106 us: attention_call(): pl.pallas_call(attention_kernel, name='attention', out_shape=(jax.ShapeDt...]
    unnamed x5 -> x0, waiting for transfers between devices: 74.5 us -> none
    dot_general x13 -> x0, matrix products: 53.3 us -> none  [the longest x1 9.28 us: local(): jnp.einsum('rd,kdc->krc', chosen, lax.all_gather(stacked, 'seq', axis=2,...]
    unnamed x43 -> x9, local copies, waits for them, and re-layouts: 55.5 us -> 6.39 us
    psum x1 -> x0, waiting for transfers between devices: 22.5 us -> none  [local(): lax.psum(grad_k.astype(jnp.bfloat16), 'dp').astype(jnp.float32)]
    convert_element_type x6 -> x0, other arithmetic: 15.6 us -> none  [the longest x1 10.9 us: attend(): unit_rms_back(query_unit, query_inverse, query_cot).astype(jnp.bfloat16)]
    reshape x2 -> x0, local copies, waits for them, and re-layouts: 12.2 us -> none  [the longest x1 6.39 us: local(): key_part.reshape(NEED, LATENTS, width)]
  transfers between devices with their start and end apart: 6 -> 0, of which waited for: 5 -> 0; matrix products, arithmetic and copies ran while one was open for 23% -> 0% of each run, Pallas kernels for 0% -> 0%
where the time goes in v1:
time: 156 us; the launch traced here: 155 us
  Pallas kernels  145 us (93%)
  local copies, waits for them, and re-layouts  9.52 us (6%)
    pallas_call x1, Pallas kernels, attention_call(): pl.pallas_call(attention_kernel, name='attention', out_shape=(jax.ShapeDt...  106 us
    pallas_call x1, Pallas kernels, gradient_call(): pl.pallas_call(gradient_kernel, name='gradients', out_shape=(jax.ShapeDty...  39.6 us
    unnamed x9, local copies, waits for them, and re-layouts  6.39 us
    slice x1, local copies, waits for them, and re-layouts, local(): d_weights[:, cols:]  3.13 us

profile of v1, /device:TPU:1, one launch (start us, length us, event | category | flops | bytes accessed | tf_op | source)
XLA Modules:
  0.0 155.5 jit_solution(3677557092518407368)
XLA Ops:
  0.6 105.7 %attention.1 = (bf16[512,4096]{1,0:T(8,128)(2,1)}, bf16[512,4096]{1,0:T(8,128)(2,1)}, bf16[1024,512]{1,0:T(8,128)(2,1)}, bf16[4,4,64,1280]{3,2,1,0:T(8,128)(2,1)}) custom-call(s32[1,16]{1,0:T(1,128)} %pos_ref.1, s32[1,16]{1,0:T(1,128)} %slot_ref.1, bf16[64,1280]{1,0:T(8,128)(2,1)} %bitcast.13, bf16[1280,256]{1,0:T(8,128)(2,1)} %kw_ref.3, ...), custom_call_target="tpu_custom_call" | custom-call | tf_op jit(solution)/shard_map/attention/pallas_call | solution.py:425
  106.4 39.6 %gradients.1 = (bf16[64,1280]{1,0:T(8,128)(2,1)}, bf16[1280,512]{1,0:T(8,128)(2,1)}) custom-call(bf16[1024,512]{1,0:T(8,128)(2,1)} %get-tuple-element.13.grad_ref, bf16[1024,1280]{1,0:T(8,128)(2,1)} %bitcast.11, bf16[1280,256]{1,0:T(8,128)(2,1)} %kw_ref.3, bf16[1280,256]{1,0:T(8,128)(2,1)} %vw_ref.3), custom_call_target="tpu_custom_call" | custom-call | tf_op jit(solution)/shard_map/gradients/pallas_call | solution.py:692
  145.9 0.0 copy-start.1
  145.9 3.1 %fusion = (f32[1280,256]{1,0:T(8,128)}, f32[1280,256]{1,0:T(8,128)}) fusion(bf16[1280,512]{1,0:T(8,128)(2,1)} %get-tuple-element.16), kind=kLoop, calls=%fused_computation | loop fusion | bytes 5242880 | tf_op jit(solution)/shard_map/slice | solution.py:745
  149.1 0.0 copy-done.1
  149.1 0.0 copy-start
  149.1 2.1 %copy.15 = bf16[1,512,4096]{2,1,0:T(8,128)(2,1)} copy(bf16[1,512,4096]{2,1,0:T(8,128)(2,1)S(1)} %bitcast.10) | data formatting | bytes 8388608
  151.2 1.6 %copy-done = bf16[512,4096]{1,0:T(8,128)(2,1)S(1)} copy-done((bf16[512,4096]{1,0:T(8,128)(2,1)S(1)}, bf16[512,4096]{1,0:T(8,128)(2,1)}, u32[]{:S(2)}) %copy-start) | copy-done | bytes 4194328
  152.8 0.0 copy-start.2
  152.8 2.0 %copy.16 = bf16[1,512,4096]{2,1,0:T(8,128)(2,1)} copy(bf16[1,512,4096]{2,1,0:T(8,128)(2,1)S(1)} %bitcast.9) | data formatting | bytes 8388608
  154.8 0.0 copy-done.2
  154.8 0.7 copy.17
Async XLA Ops:
  145.9 3.1 %copy-start.1 = (bf16[512,4096]{1,0:T(8,128)(2,1)S(1)}, bf16[512,4096]{1,0:T(8,128)(2,1)}, u32[]{:S(2)}) copy-start(bf16[512,4096]{1,0:T(8,128)(2,1)} %get-tuple-element.11) | copy-start | bytes 12582916
  149.1 3.7 %copy-start = (bf16[512,4096]{1,0:T(8,128)(2,1)S(1)}, bf16[512,4096]{1,0:T(8,128)(2,1)}, u32[]{:S(2)}) copy-start(bf16[512,4096]{1,0:T(8,128)(2,1)} %get-tuple-element.12) | copy-start | bytes 12582916
  152.8 2.0 %copy-start.2 = (bf16[64,1280]{1,0:T(8,128)(2,1)S(1)}, bf16[64,1280]{1,0:T(8,128)(2,1)}, u32[]{:S(2)}) copy-start(bf16[64,1280]{1,0:T(8,128)(2,1)} %get-tuple-element.15) | copy-start | bytes 491524

commit v2 on v0

v2 whole, which is shorter than its diff:
```python
import math

import jax
import jax.numpy as jnp
from jax import lax
from jax.experimental import pallas as pl
from jax.experimental.pallas import tpu as pltpu
from jax.sharding import PartitionSpec as P

HD = 128
LATENTS = 64
NEED = 3
SIDE = 4
SEQ = 16
ROWS = NEED * LATENTS
EPSILON = 1e-06
SCALE = 1.0 / math.sqrt(HD)
MESH = pl.DeviceIdType.MESH
F32 = jnp.float32
BF16 = jnp.bfloat16

OFFSETS = (
    (0, 0),
    (1, 0),
    (3, 0),
    (0, 1),
    (0, 3),
    (2, 0),
    (0, 2),
    (1, 1),
    (3, 3),
    (1, 3),
    (3, 1),
    (2, 1),
    (1, 2),
    (2, 3),
    (3, 2),
    (2, 2),
)
X_CODE = sum(o[0] << (2 * i) for i, o in enumerate(OFFSETS[1:]))
Y_CODE = sum(o[1] << (2 * i) for i, o in enumerate(OFFSETS[1:]))


def offset_of(step):
    place = 2 * lax.rem(step + SEQ - 1, SEQ)
    return (
        lax.rem(lax.shift_right_logical(jnp.int32(X_CODE), place), SIDE),
        lax.rem(lax.shift_right_logical(jnp.int32(Y_CODE), place), SIDE),
    )


def nt(a, b):
    return lax.dot_general(a, b, (((1,), (1,)), ((), ())), preferred_element_type=F32)


def tn(a, b):
    return lax.dot_general(a, b, (((0,), (0,)), ((), ())), preferred_element_type=F32)


def nn(a, b):
    return lax.dot_general(a, b, (((1,), (0,)), ((), ())), preferred_element_type=F32)


def mean_last(a):
    return jnp.mean(a, axis=-1, keepdims=True)


def attend_half(query, cotangent, keys, values, image):
    raw = query.astype(F32)
    inverse = lax.rsqrt(mean_last(raw * raw) + EPSILON)
    unit = raw * inverse
    unit_b = unit.astype(BF16)
    is0, is1, is2 = image == 0, image == 1, image == 2

    def choose(wide):
        return jnp.where(
            is0, wide[:LATENTS], jnp.where(is1, wide[LATENTS : 2 * LATENTS], wide[2 * LATENTS :])
        )

    def widen(narrow):
        return jnp.concatenate(
            [jnp.where(own, narrow, 0.0).astype(BF16) for own in (is0, is1, is2)], axis=0
        )

    exponent = jnp.exp(choose(nt(keys, unit_b)) * SCALE)
    probs = exponent * (1.0 / jnp.sum(exponent, axis=0, keepdims=True))
    dprob = choose(nt(values, cotangent))
    dscore = probs * (dprob - jnp.sum(probs * dprob, axis=0, keepdims=True)) * SCALE
    probs_wide = widen(probs)
    dscore_wide = widen(dscore)
    context = tn(probs_wide, values)
    query_cot = tn(dscore_wide, keys)
    d_query = inverse * (query_cot - unit * mean_last(query_cot * unit))
    return (
        context.astype(BF16),
        d_query.astype(BF16),
        nn(dscore_wide, unit_b),
        nn(probs_wide, cotangent),
    )


def whole_kernel(
    pos_ref, slot_ref, lat_ref, kw_ref, vw_ref, q_hbm, c_hbm,
    ctx_hbm, dq_hbm, dlat_ref, dk_hbm, dv_hbm,
    lat_all, lat_t, w_ref, w_t, unit_ref, inv_ref, kv_ref, kv_send, kv_recv, g_send, g_recv, run_ref, grad_ref, img_ref,
    q_buf, c_buf, first_ref, last_ref, keep_ref,
    dw_send, core_recv, z_send, z_recv, final_ref,
    da_send, db_send, da_recv, db_recv, ea_send, eb_send, ea_recv, eb_recv,
    l_ss, l_rs, f_ss, f_rs, b_ss, b_rs, q_sem, c_sem, ctx_sem, dq_sem,
    core_ss, core_rs, z_ss, z_rs, g_ss, g_rs, h_ss, h_rs, d_ss, d_rs, out_sem,
):
    tokens = q_hbm.shape[0]
    model = lat_ref.shape[1]
    cols = kw_ref.shape[1]
    heads = cols // HD
    pair = 2 * HD
    half = model // 2
    piece = half // SIDE
    group = SIDE * LATENTS
    peers = (1, 3, 2)
    dp = lax.axis_index("dp")
    me = lax.axis_index("seq")
    mx = lax.div(me, SIDE)
    my = lax.rem(me, SIDE)
    mz = lax.div(dp, 2)
    core = lax.rem(dp, 2)

    def ring(base, d):
        return lax.rem(base + d, SIDE)

    def peer(dx, dy):
        return (dp, ring(mx, dx) * SIDE + ring(my, dy))

    def z_peer(d):
        return (ring(mz, d) * 2 + core, me)

    core_peer = (mz * 2 + 1 - core, me)

    def owner_of(step):
        dx, dy = offset_of(step)
        return ring(mx, SIDE - dx) * SIDE + ring(my, SIDE - dy)

    def remote(src, dst, send_sem, recv_sem, device):
        return pltpu.make_async_remote_copy(
            src_ref=src,
            dst_ref=dst,
            send_sem=send_sem,
            recv_sem=recv_sem,
            device_id=device,
            device_id_type=MESH,
        )

    def lanes_of(n):
        place = owner_of(lax.rem(n, SEQ)) * cols + lax.div(n, SEQ) * HD
        return pl.ds(pl.multiple_of(place, HD), HD)

    def q_copy(n):
        return pltpu.make_async_copy(q_hbm.at[:, lanes_of(n)], q_buf.at[n], q_sem.at[n])

    def c_copy(n):
        return pltpu.make_async_copy(c_hbm.at[:, lanes_of(n)], c_buf.at[n], c_sem.at[n])

    def ctx_copy(n):
        return pltpu.make_async_copy(c_buf.at[n], ctx_hbm.at[:, lanes_of(n)], ctx_sem.at[n])

    def dq_copy(n):
        return pltpu.make_async_copy(q_buf.at[n], dq_hbm.at[:, lanes_of(n)], dq_sem.at[n])

    barrier = pltpu.get_barrier_semaphore()
    for dx, dy in OFFSETS[1:]:
        pl.semaphore_signal(barrier, inc=1, device_id=peer(dx, dy), device_id_type=MESH)
    for d in peers:
        pl.semaphore_signal(barrier, inc=1, device_id=z_peer(d), device_id_type=MESH)
    pl.semaphore_signal(barrier, inc=1, device_id=core_peer, device_id_type=MESH)

    low = pl.ds(0, LATENTS // 2)
    high = pl.ds(LATENTS // 2, LATENTS // 2)

    def x_first(d):
        return remote(
            lat_ref.at[low], lat_all.at[mx, my, low], l_ss.at[0, d], l_rs.at[0, d], peer(d, 0)
        )

    def y_first(d):
        return remote(
            lat_ref.at[high], lat_all.at[mx, my, high], l_ss.at[1, d], l_rs.at[1, d], peer(0, d)
        )

    def y_second(d):
        block = lat_all.at[:, my, low]
        return remote(block, block, l_ss.at[2, d], l_rs.at[2, d], peer(0, d))

    def x_second(d):
        block = lat_all.at[mx, :, high]
        return remote(block, block, l_ss.at[3, d], l_rs.at[3, d], peer(d, 0))

    lat_all[mx, my] = lat_ref[...]
    pl.semaphore_wait(barrier, SEQ - 1 + SIDE)
    for d in peers:
        x_first(d).start()
        y_first(d).start()

    def fetch(n, carry):
        q_copy(n).start()
        c_copy(n).start()
        return carry

    lax.fori_loop(0, heads * SEQ, fetch, 0)

    for head in range(heads):
        lanes = slice(head * HD, (head + 1) * HD)
        w_ref[:, head * pair : head * pair + HD] = kw_ref[:, lanes]
        w_ref[:, head * pair + HD : (head + 1) * pair] = vw_ref[:, lanes]

    def block_images(block, carry):
        count = jnp.int32(-1)
        for i in range(SEQ):
            count = count + (pos_ref[0, i] <= block * tokens).astype(jnp.int32)
        first_ref[block] = count
        return carry

    lax.fori_loop(0, SEQ, block_images, 0)

    def slot_last(slot, carry):
        image = jnp.int32(0)
        for i in range(SEQ):
            image = image + jnp.where(slot_ref[0, i] == slot, i, 0)
        image = jnp.minimum(image, SEQ - 1)
        after = pos_ref[0, jnp.minimum(image + 1, SEQ - 1)]
        end = jnp.where(image == SEQ - 1, SEQ * tokens, after) - 1
        block = jnp.maximum(lax.div(end, tokens), 0)
        place = jnp.clip(image - first_ref[block], 0, NEED - 1)
        last_ref[slot] = block * NEED + place
        return carry

    lax.fori_loop(0, SEQ, slot_last, 0)

    token = me * tokens + lax.broadcasted_iota(jnp.int32, (1, tokens), 1)
    seen = jnp.zeros((1, tokens), jnp.int32) - 1 - first_ref[me]
    for i in range(SEQ):
        seen = seen + (token >= pos_ref[0, i]).astype(jnp.int32)
    img_ref[...] = seen

    for d in peers:
        x_first(d).wait_recv()
    for d in peers:
        y_second(d).start()
    for d in peers:
        y_first(d).wait_recv()
    for d in peers:
        x_second(d).start()
    for d in peers:
        y_second(d).wait_recv()
        x_second(d).wait_recv()

    def project(x, carry):
        rows = pl.ds(pl.multiple_of(x * group, group), group)
        slots = pl.ds(x * SIDE, SIDE)
        raw = nn(lat_all[x].reshape(group, model), w_ref[...])
        for head in range(heads):
            one = raw[:, head * pair : head * pair + HD]
            inverse = lax.rsqrt(mean_last(one * one) + EPSILON)
            unit = one * inverse
            unit_ref[head, rows, :] = unit
            inv_ref[head, rows, :] = jnp.broadcast_to(inverse, unit.shape)
            kv_ref[slots, :, head * pair : head * pair + HD] = unit.astype(BF16).reshape(
                SIDE, LATENTS, HD
            )
            values = raw[:, head * pair + HD : (head + 1) * pair].astype(BF16)
            kv_ref[slots, :, head * pair + HD : (head + 1) * pair] = values.reshape(
                SIDE, LATENTS, HD
            )
        return carry

    lax.fori_loop(0, SIDE, project, 0)

    def forward(n):
        dx, dy = offset_of(lax.rem(n, SEQ))
        return remote(kv_send.at[n], kv_recv.at[n], f_ss.at[n], f_rs.at[n], peer(dx, dy))

    def backward(n):
        place = lax.div(n, SEQ) * SEQ + me
        return remote(
            g_send.at[n],
            g_recv.at[place],
            b_ss.at[n],
            b_rs.at[place],
            (dp, owner_of(lax.rem(n, SEQ))),
        )

    def arrival(n):
        return remote(g_send.at[0], g_recv.at[n], b_ss.at[0], b_rs.at[n], (dp, lax.rem(n, SEQ)))

    def prepare(target, n, head, block):
        for j in range(NEED):
            slot = slot_ref[0, jnp.minimum(first_ref[block] + j, SEQ - 1)]
            both = kv_ref[slot]
            target[n, j * LATENTS : (j + 1) * LATENTS, :] = both[:, head * pair : (head + 1) * pair]

    for head in range(heads):

        def send(step, carry, head=head):
            n = head * SEQ + step
            dx, dy = offset_of(step)
            prepare(kv_send, n, head, peer(dx, dy)[1])
            forward(n).start()
            return carry

        lax.fori_loop(1, SEQ, send, 0)
    for head in range(heads):
        prepare(kv_recv, head * SEQ, head, me)

    def turn(x, carry):
        rows = pl.ds(pl.multiple_of(x * group, group), group)
        lat_t[:, rows] = lat_all[x].reshape(group, model).T
        return carry

    lax.fori_loop(0, SIDE, turn, 0)
    w_t[...] = w_ref[...].T

    def keep_flags(block, carry):
        first = first_ref[block]
        end = (block + 1) * tokens - 1
        before = block * tokens - 1
        last = jnp.int32(-1)
        previous = jnp.int32(-1)
        for i in range(SEQ):
            last = last + (pos_ref[0, i] <= end).astype(jnp.int32)
            previous = previous + (pos_ref[0, i] <= before).astype(jnp.int32)
        for j in range(NEED):
            same = previous == first if j == 0 else first + j > last
            keep_ref[block * NEED + j] = same.astype(jnp.int32)
        return carry

    lax.fori_loop(0, SEQ, keep_flags, 0)

    def attend(n, carry):
        own = lax.rem(n, SEQ) == 0

        @pl.when(jnp.logical_not(own))
        def _():
            forward(n).wait_recv()

        q_copy(n).wait()
        c_copy(n).wait()
        keys = kv_recv[n, :, :HD]
        values = kv_recv[n, :, HD:]
        key_part = jnp.zeros((ROWS, HD), F32)
        value_part = jnp.zeros((ROWS, HD), F32)
        size = 256
        for begin in range(0, tokens, size):
            rows = slice(begin, begin + size)
            context, d_query, key_add, value_add = attend_half(
                q_buf[n, rows, :], c_buf[n, rows, :], keys, values, img_ref[:, rows]
            )
            c_buf[n, rows, :] = context
            q_buf[n, rows, :] = d_query
            key_part = key_part + key_add
            value_part = value_part + value_add
        g_send[n, :, :HD] = key_part.astype(BF16)
        g_send[n, :, HD:] = value_part.astype(BF16)

        @pl.when(jnp.logical_not(own))
        def _():
            backward(n).start()

        @pl.when(own)
        def _():
            g_recv[lax.div(n, SEQ) * SEQ + me] = g_send[n]

        ctx_copy(n).start()
        dq_copy(n).start()
        return carry

    lax.fori_loop(0, heads * SEQ, attend, 0)

    def key_value_grads(head):
        def combine(block, run):
            @pl.when(block != me)
            def _():
                arrival(head * SEQ + block).wait_recv()

            for j in range(NEED):
                keep = keep_ref[block * NEED + j].astype(F32)
                part = g_recv[head * SEQ + block, j * LATENTS : (j + 1) * LATENTS, :]
                run = run * keep + part.astype(F32)
                run_ref[block * NEED + j] = run
            return run

        lax.fori_loop(0, SEQ, combine, jnp.zeros((LATENTS, pair), F32))

        def finish(x, carry):
            rows = pl.ds(pl.multiple_of(x * group, group), group)
            total = jnp.concatenate([run_ref[last_ref[x * SIDE + y]] for y in range(SIDE)], axis=0)
            cot = total[:, :HD]
            unit = unit_ref[head, rows, :]
            key_grad = inv_ref[head, rows, :] * (cot - unit * mean_last(cot * unit))
            shape = (SIDE, LATENTS, HD)
            lanes = slice(head * pair, head * pair + HD)
            grad_ref[x, :, :, lanes] = key_grad.astype(BF16).reshape(shape)
            lanes = slice(head * pair + HD, (head + 1) * pair)
            grad_ref[x, :, :, lanes] = total[:, HD:].astype(BF16).reshape(shape)
            return carry

        lax.fori_loop(0, SIDE, finish, 0)

    own_rows = pl.multiple_of(core * half, half)
    other_rows = pl.multiple_of((1 - core) * half, half)

    def weight_grad(head, base):
        chunk = half // 2

        def one(i, carry):
            rows = pl.ds(pl.multiple_of(base + i * chunk, chunk), chunk)
            grads = grad_ref[:, :, :, head * pair : (head + 1) * pair]
            grads = grads.reshape(SEQ * LATENTS, pair)
            dw_send[head, rows, :] = nn(lat_t[rows, :], grads).astype(BF16)
            return carry

        lax.fori_loop(0, half // chunk, one, 0)

    def core_copy(head):
        return remote(
            dw_send.at[head, pl.ds(other_rows, half)],
            core_recv.at[head],
            core_ss.at[head],
            core_rs.at[head],
            core_peer,
        )

    def z_copy(head, d):
        rows = pl.ds(pl.multiple_of(ring(mz, d) * piece, piece), piece)
        return remote(
            z_send.at[head, rows],
            z_recv.at[head, d - 1],
            z_ss.at[head, d],
            z_rs.at[head, d],
            z_peer(d),
        )

    def final_rows(z, c):
        return pl.ds(pl.multiple_of(c * half + z * piece, piece), piece)

    def g_copy(head, d):
        block = final_ref.at[head, final_rows(mz, core)]
        return remote(block, block, g_ss.at[head, d], g_rs.at[head, d], z_peer(d))

    def h_copy(head, d):
        block = final_ref.at[head, final_rows(ring(mz, SIDE - d), core)]
        return remote(block, block, h_ss.at[head, d], h_rs.at[head, d], core_peer)

    def core_sum(head):
        core_copy(head).wait_recv()

        def one(i, carry):
            rows = pl.ds(pl.multiple_of(i * piece, piece), piece)
            own = pl.ds(pl.multiple_of(own_rows + i * piece, piece), piece)
            total = dw_send[head, own, :].astype(F32) + core_recv[head, rows, :].astype(F32)
            z_send[head, rows, :] = total.astype(BF16)
            return carry

        lax.fori_loop(0, SIDE, one, 0)
        for d in peers:
            z_copy(head, d).start()

    def z_sum(head):
        for d in peers:
            z_copy(head, d).wait_recv()
        total = z_send[head, pl.ds(pl.multiple_of(mz * piece, piece), piece), :].astype(F32)
        for d in peers:
            total = total + z_recv[head, d - 1].astype(F32)
        final_ref[head, final_rows(mz, core), :] = total.astype(BF16)
        for d in peers:
            g_copy(head, d).start()
        h_copy(head, 0).start()

    def hand_over(head):
        for d in peers:
            g_copy(head, d).wait_recv()
            h_copy(head, d).start()

    def out_copy(head, i):
        lanes = pl.ds(head * HD, HD)
        return pltpu.make_async_copy(
            final_ref.at[head, :, pl.ds(i * HD, HD)],
            (dk_hbm, dv_hbm)[i].at[:, lanes],
            out_sem.at[head, i],
        )

    def weight_out(head):
        for d in range(SIDE):
            h_copy(head, d).wait_recv()
        for i in range(2):
            out_copy(head, i).start()

    def da_copy(d):
        return remote(
            da_send.at[ring(mx, d)], da_recv.at[d - 1], d_ss.at[0, d], d_rs.at[0, d], peer(d, 0)
        )

    def db_copy(d):
        return remote(
            db_send.at[ring(my, d)], db_recv.at[d - 1], d_ss.at[1, d], d_rs.at[1, d], peer(0, d)
        )

    def ea_copy(d):
        return remote(
            ea_send.at[ring(my, d)], ea_recv.at[d - 1], d_ss.at[2, d], d_rs.at[2, d], peer(0, d)
        )

    def eb_copy(d):
        return remote(
            eb_send.at[ring(mx, d)], eb_recv.at[d - 1], d_ss.at[3, d], d_rs.at[3, d], peer(d, 0)
        )

    def latent_grads(i, carry):
        d = lax.rem(i + 1, SIDE)
        x = ring(mx, d)
        y = ring(my, d)
        shape = (SIDE, LATENTS, half)
        grads = grad_ref[x].reshape(group, heads * pair)
        da_send[x] = nn(grads, w_t[:, :half]).astype(BF16).reshape(shape)

        @pl.when(d > 0)
        def _():
            da_copy(d).start()

        grads = grad_ref[:, y].reshape(group, heads * pair)
        db_send[y] = nn(grads, w_t[:, half:]).astype(BF16).reshape(shape)

        @pl.when(d > 0)
        def _():
            db_copy(d).start()

        return carry

    def sum_a(y, carry):
        total = da_send[mx, y].astype(F32)
        for d in peers:
            total = total + da_recv[d - 1, y].astype(F32)
        ea_send[y] = total.astype(BF16)
        return carry

    def sum_b(x, carry):
        total = db_send[my, x].astype(F32)
        for d in peers:
            total = total + db_recv[d - 1, x].astype(F32)
        eb_send[x] = total.astype(BF16)
        return carry

    key_value_grads(0)
    weight_grad(0, other_rows)
    core_copy(0).start()
    weight_grad(0, own_rows)
    core_sum(0)
    z_sum(0)

    key_value_grads(1)
    lax.fori_loop(0, SIDE, latent_grads, 0)
    weight_grad(1, other_rows)
    core_copy(1).start()
    hand_over(0)
    weight_grad(1, own_rows)
    core_sum(1)
    for d in peers:
        da_copy(d).wait_recv()
    lax.fori_loop(0, SIDE, sum_a, 0)
    for d in peers:
        ea_copy(d).start()
    z_sum(1)
    for d in peers:
        db_copy(d).wait_recv()
    lax.fori_loop(0, SIDE, sum_b, 0)
    for d in peers:
        eb_copy(d).start()
    weight_out(0)
    hand_over(1)
    for d in peers:
        ea_copy(d).wait_recv()
    total = ea_send[my].astype(F32)
    for d in peers:
        total = total + ea_recv[d - 1].astype(F32)
    dlat_ref[:, :half] = total.astype(BF16)
    for d in peers:
        eb_copy(d).wait_recv()
    total = eb_send[mx].astype(F32)
    for d in peers:
        total = total + eb_recv[d - 1].astype(F32)
    dlat_ref[:, half:] = total.astype(BF16)
    weight_out(1)

    for d in peers:
        for copy in (x_first(d), y_first(d), x_second(d), y_second(d)):
            copy.wait_send()
        for copy in (da_copy(d), db_copy(d), ea_copy(d), eb_copy(d)):
            copy.wait_send()
        for head in range(heads):
            z_copy(head, d).wait_send()
            g_copy(head, d).wait_send()
    for head in range(heads):
        for i in range(2):
            out_copy(head, i).wait()
        core_copy(head).wait_send()
        for d in range(SIDE):
            h_copy(head, d).wait_send()

    def drain(n, carry):
        @pl.when(lax.rem(n, SEQ) > 0)
        def _():
            forward(n).wait_send()
            backward(n).wait_send()

        ctx_copy(n).wait()
        dq_copy(n).wait()
        return carry

    lax.fori_loop(0, heads * SEQ, drain, 0)


def whole_call(positions, slots, latents, k_weight, v_weight, queries, cotangents):
    tokens, width = queries.shape
    model, cols = k_weight.shape
    heads = cols // HD
    steps = heads * SEQ
    pair = 2 * HD
    half = model // 2
    piece = half // SIDE
    others = SIDE - 1
    smem = pl.BlockSpec(memory_space=pltpu.SMEM)
    vmem = pl.BlockSpec(memory_space=pltpu.VMEM)
    hbm = pl.BlockSpec(memory_space=pl.ANY)
    dma = pltpu.SemaphoreType.DMA
    return pl.pallas_call(
        whole_kernel,
        name="whole",
        out_shape=(
            jax.ShapeDtypeStruct((tokens, width), BF16),
            jax.ShapeDtypeStruct((tokens, width), BF16),
            jax.ShapeDtypeStruct((LATENTS, model), BF16),
            jax.ShapeDtypeStruct((model, cols), BF16),
            jax.ShapeDtypeStruct((model, cols), BF16),
        ),
        in_specs=[smem, smem, vmem, vmem, vmem, hbm, hbm],
        out_specs=(hbm, hbm, vmem, hbm, hbm),
        scratch_shapes=[
            pltpu.VMEM((SIDE, SIDE, LATENTS, model), BF16),
            pltpu.VMEM((model, SEQ * LATENTS), BF16),
            pltpu.VMEM((model, heads * pair), BF16),
            pltpu.VMEM((heads * pair, model), BF16),
            pltpu.VMEM((heads, SEQ * LATENTS, HD), F32),
            pltpu.VMEM((heads, SEQ * LATENTS, HD), F32),
            pltpu.VMEM((SEQ, LATENTS, heads * pair), BF16),
            pltpu.VMEM((steps, ROWS, pair), BF16),
            pltpu.VMEM((steps, ROWS, pair), BF16),
            pltpu.VMEM((steps, ROWS, pair), BF16),
            pltpu.VMEM((steps, ROWS, pair), BF16),
            pltpu.VMEM((SEQ * NEED, LATENTS, pair), F32),
            pltpu.VMEM((SIDE, SIDE, LATENTS, heads * pair), BF16),
            pltpu.VMEM((1, tokens), jnp.int32),
            pltpu.VMEM((steps, tokens, HD), BF16),
            pltpu.VMEM((steps, tokens, HD), BF16),
            pltpu.SMEM((SEQ,), jnp.int32),
            pltpu.SMEM((SEQ,), jnp.int32),
            pltpu.SMEM((SEQ * NEED,), jnp.int32),
            pltpu.VMEM((heads, model, pair), BF16),
            pltpu.VMEM((heads, half, pair), BF16),
            pltpu.VMEM((heads, half, pair), BF16),
            pltpu.VMEM((heads, others, piece, pair), BF16),
            pltpu.VMEM((heads, model, pair), BF16),
            pltpu.VMEM((SIDE, SIDE, LATENTS, half), BF16),
            pltpu.VMEM((SIDE, SIDE, LATENTS, half), BF16),
            pltpu.VMEM((others, SIDE, LATENTS, half), BF16),
            pltpu.VMEM((others, SIDE, LATENTS, half), BF16),
            pltpu.VMEM((SIDE, LATENTS, half), BF16),
            pltpu.VMEM((SIDE, LATENTS, half), BF16),
            pltpu.VMEM((others, LATENTS, half), BF16),
            pltpu.VMEM((others, LATENTS, half), BF16),
            dma((4, SIDE)),
            dma((4, SIDE)),
            dma((steps,)),
            dma((steps,)),
            dma((steps,)),
            dma((steps,)),
            dma((steps,)),
            dma((steps,)),
            dma((steps,)),
            dma((steps,)),
            dma((heads,)),
            dma((heads,)),
            dma((heads, SIDE)),
            dma((heads, SIDE)),
            dma((heads, SIDE)),
            dma((heads, SIDE)),
            dma((heads, SIDE)),
            dma((heads, SIDE)),
            dma((4, SIDE)),
            dma((4, SIDE)),
            dma((heads, 2)),
        ],
        compiler_params=pltpu.CompilerParams(
            collective_id=0, has_side_effects=True, vmem_limit_bytes=58 * 2**20
        ),
    )(positions, slots, latents, k_weight, v_weight, queries, cotangents)


def finish_kernel(
    ctx_in, dq_in, dk_in, dv_in, ctx_out, dq_out, dk_out, dv_out,
    ctx_buf, dq_buf, narrow, wide, in_sem, w_sem, load_sem, store_sem,
):
    parts = load_sem.shape[1]
    size = ctx_in.shape[0] // parts
    ends = ((ctx_in, ctx_buf, ctx_out), (dq_in, dq_buf, dq_out))

    def load_part(i, j):
        rows = pl.ds(i * size, size)
        src, dst, _ = ends[j]
        return pltpu.make_async_copy(src.at[rows], dst.at[rows], load_sem.at[j, i])

    def store_part(i, j):
        rows = pl.ds(i * size, size)
        _, src, dst = ends[j]
        return pltpu.make_async_copy(src.at[rows], dst.at[rows], store_sem.at[j, i])

    loads = [
        pltpu.make_async_copy(src, narrow.at[i], in_sem.at[i])
        for i, src in enumerate((dk_in, dv_in))
    ]
    stores = [
        pltpu.make_async_copy(wide.at[i], dst, w_sem.at[i]) for i, dst in enumerate((dk_out, dv_out))
    ]
    for load in loads:
        load.start()
    for i in range(parts):
        for j in range(2):
            load_part(i, j).start()
    for i in range(2):
        loads[i].wait()
        wide[i] = narrow[i].astype(F32)
        stores[i].start()
    for i in range(parts):
        for j in range(2):
            load_part(i, j).wait()
            store_part(i, j).start()
    for i in range(parts):
        for j in range(2):
            store_part(i, j).wait()
    for store in stores:
        store.wait()


def finish_call(context, d_queries, d_k, d_v):
    hbm = pl.BlockSpec(memory_space=pl.ANY)
    dma = pltpu.SemaphoreType.DMA
    return pl.pallas_call(
        finish_kernel,
        name="finish",
        out_shape=(
            jax.ShapeDtypeStruct(context.shape, BF16),
            jax.ShapeDtypeStruct(d_queries.shape, BF16),
            jax.ShapeDtypeStruct(d_k.shape, F32),
            jax.ShapeDtypeStruct(d_v.shape, F32),
        ),
        in_specs=[hbm] * 4,
        out_specs=(hbm,) * 4,
        scratch_shapes=[
            pltpu.VMEM(context.shape, BF16),
            pltpu.VMEM(context.shape, BF16),
            pltpu.VMEM((2, *d_k.shape), BF16),
            pltpu.VMEM((2, *d_k.shape), F32),
            dma((2,)),
            dma((2,)),
            dma((2, 8)),
            dma((2, 8)),
        ],
        compiler_params=pltpu.CompilerParams(vmem_limit_bytes=60 * 2**20),
    )(context, d_queries, d_k, d_v)


def local(queries, latents, k_weight, v_weight, d_context, image_pos, image_slot):
    context, d_queries, d_latents, d_k, d_v = whole_call(
        image_pos, image_slot, latents[0, 0], k_weight, v_weight, queries[0], d_context[0]
    )
    context, d_queries, d_k, d_v = finish_call(context, d_queries, d_k, d_v)
    return context[None], d_queries[None], d_latents[None, None], d_k, d_v


def solution(mesh):
    in_specs = (
        P("dp", "seq", None),
        P("dp", "seq", None, None),
        P(None, "seq"),
        P(None, "seq"),
        P("dp", "seq", None),
        P("dp", None),
        P("dp", None),
    )
    out_specs = (
        P("dp", "seq", None),
        P("dp", "seq", None),
        P("dp", "seq", None, None),
        P(None, "seq"),
        P(None, "seq"),
    )
    return jax.shard_map(local, mesh=mesh, in_specs=in_specs, out_specs=out_specs, check_vma=False)
```

time: 491 us -> 145 us (0.30); the launches traced: 482 us -> 143 us
  waiting for transfers between devices: 267 us -> 0 us
  Pallas kernels: 0 us -> 141 us
  local copies, waits for them, and re-layouts: 93.4 us -> 0.67 us
  matrix products: 58.5 us -> 0 us
  other arithmetic: 36.9 us -> 0 us
  between operations: 14.7 us -> 0.67 us
  starting transfers between devices: 11.5 us -> 0 us
    all_gather x2 -> x0, waiting for transfers between devices: 166 us -> none  [the longest x1 138 us: local(): lax.all_gather(stacked, 'seq', axis=2, tiled=True)]
    pallas_call x0 -> x2, Pallas kernels: none -> 141 us  [the longest x1 133 us: whole_call(): pl.pallas_call(whole_kernel, name='whole', out_shape=(jax.ShapeDtypeStruc...]
    unnamed x5 -> x0, waiting for transfers between devices: 74.5 us -> none
    unnamed x43 -> x3, local copies, waits for them, and re-layouts: 55.5 us -> 0.67 us
    dot_general x13 -> x0, matrix products: 53.3 us -> none  [the longest x1 9.28 us: local(): jnp.einsum('rd,kdc->krc', chosen, lax.all_gather(stacked, 'seq', axis=2,...]
    psum x1 -> x0, waiting for transfers between devices: 22.5 us -> none  [local(): lax.psum(grad_k.astype(jnp.bfloat16), 'dp').astype(jnp.float32)]
    convert_element_type x6 -> x0, other arithmetic: 15.6 us -> none  [the longest x1 10.9 us: attend(): unit_rms_back(query_unit, query_inverse, query_cot).astype(jnp.bfloat16)]
    reshape x2 -> x0, local copies, waits for them, and re-layouts: 12.2 us -> none  [the longest x1 6.39 us: local(): key_part.reshape(NEED, LATENTS, width)]
  transfers between devices with their start and end apart: 6 -> 0, of which waited for: 5 -> 0; matrix products, arithmetic and copies ran while one was open for 23% -> 0% of each run, Pallas kernels for 0% -> 0%
where the time goes in v2:
time: 145 us; the launch traced here: 143 us
  Pallas kernels  141 us (97%)
    pallas_call x1, Pallas kernels, whole_call(): pl.pallas_call(whole_kernel, name='whole', out_shape=(jax.ShapeDtypeStruc...  133 us
    pallas_call x1, Pallas kernels, finish_call(): pl.pallas_call(finish_kernel, name='finish', out_shape=(jax.ShapeDtypeStr...  7.77 us

profile of v2, /device:TPU:1, one launch (start us, length us, event | category | flops | bytes accessed | tf_op | source)
XLA Modules:
  0.0 142.6 jit_solution(11626167894416741978)
XLA Ops:
  0.6 133.5 %whole.1 = (bf16[512,4096]{1,0:T(8,128)(2,1)}, bf16[512,4096]{1,0:T(8,128)(2,1)}, bf16[64,1280]{1,0:T(8,128)(2,1)}, bf16[1280,256]{1,0:T(8,128)(2,1)}, bf16[1280,256]{1,0:T(8,128)(2,1)}) custom-call(s32[1,16]{1,0:T(1,128)} %pos_ref.1, s32[1,16]{1,0:T(1,128)} %slot_ref.1, bf16[64,1280]{1,0:T(8,128)(2,1)} %bitcast.9, bf16[1280,256]{1,0:T(8,128)(2,1)} %kw_ref.1, ...), custom_call_target="tpu_custom_call" | custom-call | tf_op jit(solution)/shard_map/whole/pallas_call | solution.py:633
  134.1 0.0 copy-start
  134.1 7.8 %finish.1 = (bf16[512,4096]{1,0:T(8,128)(2,1)}, bf16[512,4096]{1,0:T(8,128)(2,1)}, f32[1280,256]{1,0:T(8,128)}, f32[1280,256]{1,0:T(8,128)}) custom-call(bf16[512,4096]{1,0:T(8,128)(2,1)} %get-tuple-element.14.ctx_in, bf16[512,4096]{1,0:T(8,128)(2,1)} %get-tuple-element.15.dq_in, bf16[1280,256]{1,0:T(8,128)(2,1)} %get-tuple-element.16.dk_in, ...), custom_call_target="tpu_custom_call" | custom-call | tf_op jit(solution)/shard_map/finish/pallas_call | solution.py:754
  141.9 0.0 copy-done
  141.9 0.7 copy.13
Async XLA Ops:
  134.1 7.8 %copy-start = (bf16[64,1280]{1,0:T(8,128)(2,1)S(1)}, bf16[64,1280]{1,0:T(8,128)(2,1)}, u32[]{:S(2)}) copy-start(bf16[64,1280]{1,0:T(8,128)(2,1)} %get-tuple-element.20) | copy-start | bytes 491524

commit v3 on v2

--- a/solution.py
+++ b/solution.py
@@ -101,13 +101,13 @@
 
 def whole_kernel(
     pos_ref, slot_ref, lat_ref, kw_ref, vw_ref, q_hbm, c_hbm,
-    ctx_hbm, dq_hbm, dlat_ref, dk_hbm, dv_hbm,
+    c_buf, q_buf, dlat_ref, dk_ref, dv_ref,
     lat_all, lat_t, w_ref, w_t, unit_ref, inv_ref, kv_ref, kv_send, kv_recv, g_send, g_recv, run_ref, grad_ref, img_ref,
-    q_buf, c_buf, first_ref, last_ref, keep_ref,
+    first_ref, last_ref, keep_ref,
     dw_send, core_recv, z_send, z_recv, final_ref,
     da_send, db_send, da_recv, db_recv, ea_send, eb_send, ea_recv, eb_recv,
-    l_ss, l_rs, f_ss, f_rs, b_ss, b_rs, q_sem, c_sem, ctx_sem, dq_sem,
-    core_ss, core_rs, z_ss, z_rs, g_ss, g_rs, h_ss, h_rs, d_ss, d_rs, out_sem,
+    l_ss, l_rs, f_ss, f_rs, b_ss, b_rs, q_sem, c_sem,
+    core_ss, core_rs, z_ss, z_rs, g_ss, g_rs, h_ss, h_rs, d_ss, d_rs,
 ):
     tokens = q_hbm.shape[0]
     model = lat_ref.shape[1]
@@ -159,12 +159,6 @@
 
     def c_copy(n):
         return pltpu.make_async_copy(c_hbm.at[:, lanes_of(n)], c_buf.at[n], c_sem.at[n])
-
-    def ctx_copy(n):
-        return pltpu.make_async_copy(c_buf.at[n], ctx_hbm.at[:, lanes_of(n)], ctx_sem.at[n])
-
-    def dq_copy(n):
-        return pltpu.make_async_copy(q_buf.at[n], dq_hbm.at[:, lanes_of(n)], dq_sem.at[n])
 
     barrier = pltpu.get_barrier_semaphore()
     for dx, dy in OFFSETS[1:]:
@@ -368,8 +362,6 @@
         def _():
             g_recv[lax.div(n, SEQ) * SEQ + me] = g_send[n]
 
-        ctx_copy(n).start()
-        dq_copy(n).start()
         return carry
 
     lax.fori_loop(0, heads * SEQ, attend, 0)
@@ -479,19 +471,19 @@
             g_copy(head, d).wait_recv()
             h_copy(head, d).start()
 
-    def out_copy(head, i):
-        lanes = pl.ds(head * HD, HD)
-        return pltpu.make_async_copy(
-            final_ref.at[head, :, pl.ds(i * HD, HD)],
-            (dk_hbm, dv_hbm)[i].at[:, lanes],
-            out_sem.at[head, i],
-        )
-
     def weight_out(head):
         for d in range(SIDE):
             h_copy(head, d).wait_recv()
-        for i in range(2):
-            out_copy(head, i).start()
+        lanes = slice(head * HD, (head + 1) * HD)
+
+        def one(i, carry):
+            rows = pl.ds(pl.multiple_of(i * piece, piece), piece)
+            both = final_ref[head, rows, :].astype(F32)
+            dk_ref[rows, lanes] = both[:, :HD]
+            dv_ref[rows, lanes] = both[:, HD:]
+            return carry
+
+        lax.fori_loop(0, 2 * SIDE, one, 0)
 
     def da_copy(d):
         return remote(
@@ -598,8 +590,6 @@
             z_copy(head, d).wait_send()
             g_copy(head, d).wait_send()
     for head in range(heads):
-        for i in range(2):
-            out_copy(head, i).wait()
         core_copy(head).wait_send()
         for d in range(SIDE):
             h_copy(head, d).wait_send()
@@ -610,8 +600,6 @@
             forward(n).wait_send()
             backward(n).wait_send()
 
-        ctx_copy(n).wait()
-        dq_copy(n).wait()
         return carry
 
     lax.fori_loop(0, heads * SEQ, drain, 0)
@@ -634,14 +622,14 @@
         whole_kernel,
         name="whole",
         out_shape=(
-            jax.ShapeDtypeStruct((tokens, width), BF16),
-            jax.ShapeDtypeStruct((tokens, width), BF16),
-            jax.ShapeDtypeStruct((LATENTS, model), BF16),
-            jax.ShapeDtypeStruct((model, cols), BF16),
-            jax.ShapeDtypeStruct((model, cols), BF16),
+            pltpu.VMEM((steps, tokens, HD), BF16),
+            pltpu.VMEM((steps, tokens, HD), BF16),
+            pltpu.VMEM((LATENTS, model), BF16),
+            pltpu.VMEM((model, cols), F32),
+            pltpu.VMEM((model, cols), F32),
         ),
         in_specs=[smem, smem, vmem, vmem, vmem, hbm, hbm],
-        out_specs=(hbm, hbm, vmem, hbm, hbm),
+        out_specs=(vmem,) * 5,
         scratch_shapes=[
             pltpu.VMEM((SIDE, SIDE, LATENTS, model), BF16),
             pltpu.VMEM((model, SEQ * LATENTS), BF16),
@@ -657,8 +645,6 @@
             pltpu.VMEM((SEQ * NEED, LATENTS, pair), F32),
             pltpu.VMEM((SIDE, SIDE, LATENTS, heads * pair), BF16),
             pltpu.VMEM((1, tokens), jnp.int32),
-            pltpu.VMEM((steps, tokens, HD), BF16),
-            pltpu.VMEM((steps, tokens, HD), BF16),
             pltpu.SMEM((SEQ,), jnp.int32),
             pltpu.SMEM((SEQ,), jnp.int32),
             pltpu.SMEM((SEQ * NEED,), jnp.int32),
@@ -683,8 +669,6 @@
             dma((steps,)),
             dma((steps,)),
             dma((steps,)),
-            dma((steps,)),
-            dma((steps,)),
             dma((heads,)),
             dma((heads,)),
             dma((heads, SIDE)),
@@ -695,92 +679,81 @@
             dma((heads, SIDE)),
             dma((4, SIDE)),
             dma((4, SIDE)),
-            dma((heads, 2)),
         ],
         compiler_params=pltpu.CompilerParams(
-            collective_id=0, has_side_effects=True, vmem_limit_bytes=58 * 2**20
+            collective_id=0, has_side_effects=True, vmem_limit_bytes=46 * 2**20
         ),
     )(positions, slots, latents, k_weight, v_weight, queries, cotangents)
 
 
 def finish_kernel(
-    ctx_in, dq_in, dk_in, dv_in, ctx_out, dq_out, dk_out, dv_out,
-    ctx_buf, dq_buf, narrow, wide, in_sem, w_sem, load_sem, store_sem,
+    ctx_in, dq_in, dk_in, dv_in, dlat_in, ctx_out, dq_out, dk_out, dv_out, dlat_out, store_sem, sem
 ):
-    parts = load_sem.shape[1]
-    size = ctx_in.shape[0] // parts
-    ends = ((ctx_in, ctx_buf, ctx_out), (dq_in, dq_buf, dq_out))
-
-    def load_part(i, j):
-        rows = pl.ds(i * size, size)
-        src, dst, _ = ends[j]
-        return pltpu.make_async_copy(src.at[rows], dst.at[rows], load_sem.at[j, i])
-
-    def store_part(i, j):
-        rows = pl.ds(i * size, size)
-        _, src, dst = ends[j]
-        return pltpu.make_async_copy(src.at[rows], dst.at[rows], store_sem.at[j, i])
-
-    loads = [
-        pltpu.make_async_copy(src, narrow.at[i], in_sem.at[i])
-        for i, src in enumerate((dk_in, dv_in))
+    cols = dk_in.shape[1]
+    me = lax.axis_index("seq")
+    mx = lax.div(me, SIDE)
+    my = lax.rem(me, SIDE)
+    plain = [
+        pltpu.make_async_copy(src, dst, sem.at[i])
+        for i, (src, dst) in enumerate(((dk_in, dk_out), (dv_in, dv_out), (dlat_in, dlat_out)))
     ]
-    stores = [
-        pltpu.make_async_copy(wide.at[i], dst, w_sem.at[i]) for i, dst in enumerate((dk_out, dv_out))
-    ]
-    for load in loads:
-        load.start()
-    for i in range(parts):
+
+    def store(n, j):
+        src, dst = ((ctx_in, ctx_out), (dq_in, dq_out))[j]
+        dx, dy = offset_of(lax.rem(n, SEQ))
+        owner = lax.rem(mx - dx + SIDE, SIDE) * SIDE + lax.rem(my - dy + SIDE, SIDE)
+        place = owner * cols + lax.div(n, SEQ) * HD
+        lanes = pl.ds(pl.multiple_of(place, HD), HD)
+        return pltpu.make_async_copy(src.at[n], dst.at[:, lanes], store_sem.at[j, n])
+
+    def start(n, carry):
         for j in range(2):
-            load_part(i, j).start()
-    for i in range(2):
-        loads[i].wait()
-        wide[i] = narrow[i].astype(F32)
-        stores[i].start()
-    for i in range(parts):
+            store(n, j).start()
+        return carry
+
+    def wait(n, carry):
         for j in range(2):
-            load_part(i, j).wait()
-            store_part(i, j).start()
-    for i in range(parts):
-        for j in range(2):
-            store_part(i, j).wait()
-    for store in stores:
-        store.wait()
-
-
-def finish_call(context, d_queries, d_k, d_v):
+            store(n, j).wait()
+        return carry
+
+    lax.fori_loop(0, ctx_in.shape[0], start, 0)
+    for copy in plain:
+        copy.start()
+    lax.fori_loop(0, ctx_in.shape[0], wait, 0)
+    for copy in plain:
+        copy.wait()
+
+
+def finish_call(context, d_queries, d_k, d_v, d_latents):
     hbm = pl.BlockSpec(memory_space=pl.ANY)
     dma = pltpu.SemaphoreType.DMA
+    steps, tokens = context.shape[:2]
+    whole = jax.ShapeDtypeStruct((tokens, steps * HD), BF16)
     return pl.pallas_call(
         finish_kernel,
         name="finish",
         out_shape=(
-            jax.ShapeDtypeStruct(context.shape, BF16),
-            jax.ShapeDtypeStruct(d_queries.shape, BF16),
+            whole,
+            whole,
             jax.ShapeDtypeStruct(d_k.shape, F32),
             jax.ShapeDtypeStruct(d_v.shape, F32),
+            jax.ShapeDtypeStruct(d_latents.shape, BF16),
         ),
-        in_specs=[hbm] * 4,
-        out_specs=(hbm,) * 4,
+        in_specs=[hbm] * 5,
+        out_specs=(hbm,) * 5,
         scratch_shapes=[
-            pltpu.VMEM(context.shape, BF16),
-            pltpu.VMEM(context.shape, BF16),
-            pltpu.VMEM((2, *d_k.shape), BF16),
-            pltpu.VMEM((2, *d_k.shape), F32),
-            dma((2,)),
-            dma((2,)),
-            dma((2, 8)),
-            dma((2, 8)),
+            dma((2, steps)),
+            dma((3,)),
         ],
-        compiler_params=pltpu.CompilerParams(vmem_limit_bytes=60 * 2**20),
-    )(context, d_queries, d_k, d_v)
+        compiler_params=pltpu.CompilerParams(vmem_limit_bytes=4 * 2**20),
+    )(context, d_queries, d_k, d_v, d_latents)
 
 
 def local(queries, latents, k_weight, v_weight, d_context, image_pos, image_slot):
     context, d_queries, d_latents, d_k, d_v = whole_call(
         image_pos, image_slot, latents[0, 0], k_weight, v_weight, queries[0], d_context[0]
     )
-    context, d_queries, d_k, d_v = finish_call(context, d_queries, d_k, d_v)
+    context, d_queries, d_k, d_v, d_latents = finish_call(context, d_queries, d_k, d_v, d_latents)
     return context[None], d_queries[None], d_latents[None, None], d_k, d_v
 
 

time: 145 us -> 139 us (0.959)
  Pallas kernels: 141 us -> 136 us
    pallas_call x2, Pallas kernels: 141 us -> 136 us  [the longest x1 131 us: whole_call(): pl.pallas_call(whole_kernel, name='whole', out_shape=(pltpu.VMEM((steps,...]
where the time goes in v3:
time: 139 us; the launch traced here: 137 us
  Pallas kernels  136 us (98%)
    pallas_call x1, Pallas kernels, whole_call(): pl.pallas_call(whole_kernel, name='whole', out_shape=(pltpu.VMEM((steps,...  131 us
    pallas_call x1, Pallas kernels, finish_call(): pl.pallas_call(finish_kernel, name='finish', out_shape=(whole, whole, jax...  4.69 us

profile of v3, /device:TPU:1, one launch (start us, length us, event | category | flops | bytes accessed | tf_op | source)
XLA Modules:
  0.0 136.7 jit_solution(2344300807075842435)
XLA Ops:
  0.6 131.3 %whole.1 = (bf16[32,512,128]{2,1,0:T(8,128)(2,1)S(1)}, bf16[32,512,128]{2,1,0:T(8,128)(2,1)S(1)}, bf16[64,1280]{1,0:T(8,128)(2,1)S(1)}, f32[1280,256]{1,0:T(8,128)S(1)}, f32[1280,256]{1,0:T(8,128)S(1)}) custom-call(s32[1,16]{1,0:T(1,128)} %pos_ref.1, s32[1,16]{1,0:T(1,128)} %slot_ref.1, bf16[64,1280]{1,0:T(8,128)(2,1)} %bitcast.8, bf16[1280,256]{1,0:T(8,128)(2,1)} %kw_ref.1, ...), custom_call_target="tpu_custom_call" | custom-call | tf_op jit(solution)/shard_map/whole/pallas_call | solution.py:621
  132.0 4.7 %finish.1 = (bf16[512,4096]{1,0:T(8,128)(2,1)}, bf16[512,4096]{1,0:T(8,128)(2,1)}, f32[1280,256]{1,0:T(8,128)}, f32[1280,256]{1,0:T(8,128)}, bf16[64,1280]{1,0:T(8,128)(2,1)}) custom-call(bf16[32,512,128]{2,1,0:T(8,128)(2,1)S(1)} %get-tuple-element.15.ctx_in, bf16[32,512,128]{2,1,0:T(8,128)(2,1)S(1)} %get-tuple-element.16.dq_in, ...), custom_call_target="tpu_custom_call" | custom-call | tf_op jit(solution)/shard_map/finish/pallas_call | solution.py:732

commit v4 on v3

--- a/solution.py
+++ b/solution.py
@@ -100,18 +100,18 @@
 
 
 def whole_kernel(
-    pos_ref, slot_ref, lat_ref, kw_ref, vw_ref, q_hbm, c_hbm,
+    pos_ref, slot_ref, lat_hbm, kw_hbm, vw_hbm, q_hbm, c_hbm,
     c_buf, q_buf, dlat_ref, dk_ref, dv_ref,
     lat_all, lat_t, w_ref, w_t, unit_ref, inv_ref, kv_ref, kv_send, kv_recv, g_send, g_recv, run_ref, grad_ref, img_ref,
     first_ref, last_ref, keep_ref,
     dw_send, core_recv, z_send, z_recv, final_ref,
     da_send, db_send, da_recv, db_recv, ea_send, eb_send, ea_recv, eb_recv,
-    l_ss, l_rs, f_ss, f_rs, b_ss, b_rs, q_sem, c_sem,
+    l_ss, l_rs, m_ss, m_rs, f_ss, f_rs, b_ss, b_rs, q_sem, in_sem,
     core_ss, core_rs, z_ss, z_rs, g_ss, g_rs, h_ss, h_rs, d_ss, d_rs,
 ):
     tokens = q_hbm.shape[0]
-    model = lat_ref.shape[1]
-    cols = kw_ref.shape[1]
+    model = lat_hbm.shape[1]
+    cols = kw_hbm.shape[1]
     heads = cols // HD
     pair = 2 * HD
     half = model // 2
@@ -154,11 +154,10 @@
         place = owner_of(lax.rem(n, SEQ)) * cols + lax.div(n, SEQ) * HD
         return pl.ds(pl.multiple_of(place, HD), HD)
 
-    def q_copy(n):
-        return pltpu.make_async_copy(q_hbm.at[:, lanes_of(n)], q_buf.at[n], q_sem.at[n])
-
-    def c_copy(n):
-        return pltpu.make_async_copy(c_hbm.at[:, lanes_of(n)], c_buf.at[n], c_sem.at[n])
+    def fetch(i, j):
+        rows = pl.ds(i * (tokens // SIDE), tokens // SIDE)
+        src, dst = ((q_hbm, q_buf), (c_hbm, c_buf))[j]
+        return pltpu.make_async_copy(src.at[rows], dst.at[rows], q_sem.at[i, j])
 
     barrier = pltpu.get_barrier_semaphore()
     for dx, dy in OFFSETS[1:]:
@@ -172,39 +171,47 @@
 
     def x_first(d):
         return remote(
-            lat_ref.at[low], lat_all.at[mx, my, low], l_ss.at[0, d], l_rs.at[0, d], peer(d, 0)
+            lat_hbm.at[low], lat_all.at[mx, my, low], l_ss.at[0, d], l_rs.at[0, d], peer(d, 0)
         )
 
     def y_first(d):
         return remote(
-            lat_ref.at[high], lat_all.at[mx, my, high], l_ss.at[1, d], l_rs.at[1, d], peer(0, d)
-        )
-
-    def y_second(d):
-        block = lat_all.at[:, my, low]
-        return remote(block, block, l_ss.at[2, d], l_rs.at[2, d], peer(0, d))
-
-    def x_second(d):
-        block = lat_all.at[mx, :, high]
-        return remote(block, block, l_ss.at[3, d], l_rs.at[3, d], peer(d, 0))
-
-    lat_all[mx, my] = lat_ref[...]
+            lat_hbm.at[high], lat_all.at[mx, my, high], l_ss.at[1, d], l_rs.at[1, d], peer(0, d)
+        )
+
+    def y_second(s, d):
+        block = lat_all.at[ring(mx, SIDE - s), my, low]
+        source = lat_hbm.at[low] if s == 0 else block
+        return remote(source, block, m_ss.at[0, s, d], m_rs.at[0, s, d], peer(0, d))
+
+    def x_second(s, d):
+        block = lat_all.at[mx, ring(my, SIDE - s), high]
+        source = lat_hbm.at[high] if s == 0 else block
+        return remote(source, block, m_ss.at[1, s, d], m_rs.at[1, s, d], peer(d, 0))
+
+    copies = [pltpu.make_async_copy(lat_hbm, lat_all.at[mx, my], in_sem.at[0])]
+    for head in range(heads):
+        for i, src in enumerate((kw_hbm, vw_hbm)):
+            copies.append(
+                pltpu.make_async_copy(
+                    src.at[:, pl.ds(head * HD, HD)],
+                    w_ref.at[:, pl.ds(head * pair + i * HD, HD)],
+                    in_sem.at[1 + 2 * head + i],
+                )
+            )
+    for copy in copies:
+        copy.start()
     pl.semaphore_wait(barrier, SEQ - 1 + SIDE)
     for d in peers:
         x_first(d).start()
         y_first(d).start()
-
-    def fetch(n, carry):
-        q_copy(n).start()
-        c_copy(n).start()
-        return carry
-
-    lax.fori_loop(0, heads * SEQ, fetch, 0)
-
-    for head in range(heads):
-        lanes = slice(head * HD, (head + 1) * HD)
-        w_ref[:, head * pair : head * pair + HD] = kw_ref[:, lanes]
-        w_ref[:, head * pair + HD : (head + 1) * pair] = vw_ref[:, lanes]
+    for d in peers:
+        y_second(0, d).start()
+        x_second(0, d).start()
+
+    for i in range(SIDE):
+        for j in range(2):
+            fetch(i, j).start()
 
     def block_images(block, carry):
         count = jnp.int32(-1)
@@ -235,17 +242,19 @@
         seen = seen + (token >= pos_ref[0, i]).astype(jnp.int32)
     img_ref[...] = seen
 
-    for d in peers:
-        x_first(d).wait_recv()
-    for d in peers:
-        y_second(d).start()
-    for d in peers:
-        y_first(d).wait_recv()
-    for d in peers:
-        x_second(d).start()
-    for d in peers:
-        y_second(d).wait_recv()
-        x_second(d).wait_recv()
+    for s in peers:
+        x_first(s).wait_recv()
+        for d in peers:
+            y_second(s, d).start()
+        y_first(s).wait_recv()
+        for d in peers:
+            x_second(s, d).start()
+    for s in (0, *peers):
+        for d in peers:
+            y_second(s, d).wait_recv()
+            x_second(s, d).wait_recv()
+    for copy in copies:
+        copy.wait()
 
     def project(x, carry):
         rows = pl.ds(pl.multiple_of(x * group, group), group)
@@ -328,6 +337,10 @@
 
     lax.fori_loop(0, SEQ, keep_flags, 0)
 
+    for i in range(SIDE):
+        for j in range(2):
+            fetch(i, j).wait()
+
     def attend(n, carry):
         own = lax.rem(n, SEQ) == 0
 
@@ -335,8 +348,7 @@
         def _():
             forward(n).wait_recv()
 
-        q_copy(n).wait()
-        c_copy(n).wait()
+        lanes = lanes_of(n)
         keys = kv_recv[n, :, :HD]
         values = kv_recv[n, :, HD:]
         key_part = jnp.zeros((ROWS, HD), F32)
@@ -345,10 +357,10 @@
         for begin in range(0, tokens, size):
             rows = slice(begin, begin + size)
             context, d_query, key_add, value_add = attend_half(
-                q_buf[n, rows, :], c_buf[n, rows, :], keys, values, img_ref[:, rows]
+                q_buf[rows, lanes], c_buf[rows, lanes], keys, values, img_ref[:, rows]
             )
-            c_buf[n, rows, :] = context
-            q_buf[n, rows, :] = d_query
+            c_buf[rows, lanes] = context
+            q_buf[rows, lanes] = d_query
             key_part = key_part + key_add
             value_part = value_part + value_add
         g_send[n, :, :HD] = key_part.astype(BF16)
@@ -485,25 +497,37 @@
 
         lax.fori_loop(0, 2 * SIDE, one, 0)
 
-    def da_copy(d):
-        return remote(
-            da_send.at[ring(mx, d)], da_recv.at[d - 1], d_ss.at[0, d], d_rs.at[0, d], peer(d, 0)
-        )
-
-    def db_copy(d):
-        return remote(
-            db_send.at[ring(my, d)], db_recv.at[d - 1], d_ss.at[1, d], d_rs.at[1, d], peer(0, d)
+    def da_copy(d, e):
+        y = ring(my, e)
+        return remote(
+            da_send.at[ring(mx, d), y],
+            da_recv.at[d - 1, y],
+            d_ss.at[0, d, e],
+            d_rs.at[0, d, e],
+            peer(d, 0),
+        )
+
+    def db_copy(d, e):
+        x = ring(mx, e)
+        return remote(
+            db_send.at[ring(my, d), x],
+            db_recv.at[d - 1, x],
+            d_ss.at[1, d, e],
+            d_rs.at[1, d, e],
+            peer(0, d),
         )
 
     def ea_copy(d):
         return remote(
-            ea_send.at[ring(my, d)], ea_recv.at[d - 1], d_ss.at[2, d], d_rs.at[2, d], peer(0, d)
+            ea_send.at[ring(my, d)], ea_recv.at[d - 1], d_ss.at[2, 0, d], d_rs.at[2, 0, d], peer(0, d)
         )
 
     def eb_copy(d):
         return remote(
-            eb_send.at[ring(mx, d)], eb_recv.at[d - 1], d_ss.at[3, d], d_rs.at[3, d], peer(d, 0)
-        )
+            eb_send.at[ring(mx, d)], eb_recv.at[d - 1], d_ss.at[3, 0, d], d_rs.at[3, 0, d], peer(d, 0)
+        )
+
+    order = (*peers, 0)
 
     def latent_grads(i, carry):
         d = lax.rem(i + 1, SIDE)
@@ -515,30 +539,43 @@
 
         @pl.when(d > 0)
         def _():
-            da_copy(d).start()
+            for e in order[:2]:
+                da_copy(d, e).start()
 
         grads = grad_ref[:, y].reshape(group, heads * pair)
         db_send[y] = nn(grads, w_t[:, half:]).astype(BF16).reshape(shape)
 
         @pl.when(d > 0)
         def _():
-            db_copy(d).start()
+            for e in order[:2]:
+                db_copy(d, e).start()
 
         return carry
 
-    def sum_a(y, carry):
+    def latent_send(e):
+        for d in peers:
+            da_copy(d, e).start()
+            db_copy(d, e).start()
+
+    def latent_step(e):
+        y = ring(my, e)
+        x = ring(mx, e)
+        for d in peers:
+            da_copy(d, e).wait_recv()
         total = da_send[mx, y].astype(F32)
         for d in peers:
             total = total + da_recv[d - 1, y].astype(F32)
         ea_send[y] = total.astype(BF16)
-        return carry
-
-    def sum_b(x, carry):
+        if e:
+            ea_copy(e).start()
+        for d in peers:
+            db_copy(d, e).wait_recv()
         total = db_send[my, x].astype(F32)
         for d in peers:
             total = total + db_recv[d - 1, x].astype(F32)
         eb_send[x] = total.astype(BF16)
-        return carry
+        if e:
+            eb_copy(e).start()
 
     key_value_grads(0)
     weight_grad(0, other_rows)
@@ -548,25 +585,21 @@
     z_sum(0)
 
     key_value_grads(1)
-    lax.fori_loop(0, SIDE, latent_grads, 0)
     weight_grad(1, other_rows)
     core_copy(1).start()
-    hand_over(0)
+    lax.fori_loop(0, SIDE, latent_grads, 0)
     weight_grad(1, own_rows)
     core_sum(1)
-    for d in peers:
-        da_copy(d).wait_recv()
-    lax.fori_loop(0, SIDE, sum_a, 0)
-    for d in peers:
-        ea_copy(d).start()
+    hand_over(0)
+    latent_step(1)
+    latent_send(2)
     z_sum(1)
-    for d in peers:
-        db_copy(d).wait_recv()
-    lax.fori_loop(0, SIDE, sum_b, 0)
-    for d in peers:
-        eb_copy(d).start()
+    latent_step(3)
+    latent_send(0)
     weight_out(0)
+    latent_step(2)
     hand_over(1)
+    latent_step(0)
     for d in peers:
         ea_copy(d).wait_recv()
     total = ea_send[my].astype(F32)
@@ -582,10 +615,15 @@
     weight_out(1)
 
     for d in peers:
-        for copy in (x_first(d), y_first(d), x_second(d), y_second(d)):
-            copy.wait_send()
-        for copy in (da_copy(d), db_copy(d), ea_copy(d), eb_copy(d)):
-            copy.wait_send()
+        x_first(d).wait_send()
+        y_first(d).wait_send()
+        ea_copy(d).wait_send()
+        eb_copy(d).wait_send()
+        for s in (0, *peers):
+            x_second(s, d).wait_send()
+            y_second(s, d).wait_send()
+            da_copy(d, s).wait_send()
+            db_copy(d, s).wait_send()
         for head in range(heads):
             z_copy(head, d).wait_send()
             g_copy(head, d).wait_send()
@@ -622,13 +660,13 @@
         whole_kernel,
         name="whole",
         out_shape=(
-            pltpu.VMEM((steps, tokens, HD), BF16),
-            pltpu.VMEM((steps, tokens, HD), BF16),
+            pltpu.VMEM((tokens, width), BF16),
+            pltpu.VMEM((tokens, width), BF16),
             pltpu.VMEM((LATENTS, model), BF16),
             pltpu.VMEM((model, cols), F32),
             pltpu.VMEM((model, cols), F32),
         ),
-        in_specs=[smem, smem, vmem, vmem, vmem, hbm, hbm],
+        in_specs=[smem, smem, hbm, hbm, hbm, hbm, hbm],
         out_specs=(vmem,) * 5,
         scratch_shapes=[
             pltpu.VMEM((SIDE, SIDE, LATENTS, model), BF16),
@@ -661,14 +699,16 @@
             pltpu.VMEM((SIDE, LATENTS, half), BF16),
             pltpu.VMEM((others, LATENTS, half), BF16),
             pltpu.VMEM((others, LATENTS, half), BF16),
-            dma((4, SIDE)),
-            dma((4, SIDE)),
+            dma((2, SIDE)),
+            dma((2, SIDE)),
+            dma((2, SIDE, SIDE)),
+            dma((2, SIDE, SIDE)),
             dma((steps,)),
             dma((steps,)),
             dma((steps,)),
             dma((steps,)),
-            dma((steps,)),
-            dma((steps,)),
+            dma((SIDE, 2)),
+            dma((1 + 2 * heads,)),
             dma((heads,)),
             dma((heads,)),
             dma((heads, SIDE)),
@@ -677,8 +717,8 @@
             dma((heads, SIDE)),
             dma((heads, SIDE)),
             dma((heads, SIDE)),
-            dma((4, SIDE)),
-            dma((4, SIDE)),
+            dma((4, SIDE, SIDE)),
+            dma((4, SIDE, SIDE)),
         ],
         compiler_params=pltpu.CompilerParams(
             collective_id=0, has_side_effects=True, vmem_limit_bytes=46 * 2**20
@@ -687,48 +727,26 @@
 
 
 def finish_kernel(
-    ctx_in, dq_in, dk_in, dv_in, dlat_in, ctx_out, dq_out, dk_out, dv_out, dlat_out, store_sem, sem
+    ctx_in, dq_in, dk_in, dv_in, dlat_in, ctx_out, dq_out, dk_out, dv_out, dlat_out, sems, lat_sem
 ):
-    cols = dk_in.shape[1]
-    me = lax.axis_index("seq")
-    mx = lax.div(me, SIDE)
-    my = lax.rem(me, SIDE)
-    plain = [
-        pltpu.make_async_copy(src, dst, sem.at[i])
-        for i, (src, dst) in enumerate(((dk_in, dk_out), (dv_in, dv_out), (dlat_in, dlat_out)))
-    ]
-
-    def store(n, j):
-        src, dst = ((ctx_in, ctx_out), (dq_in, dq_out))[j]
-        dx, dy = offset_of(lax.rem(n, SEQ))
-        owner = lax.rem(mx - dx + SIDE, SIDE) * SIDE + lax.rem(my - dy + SIDE, SIDE)
-        place = owner * cols + lax.div(n, SEQ) * HD
-        lanes = pl.ds(pl.multiple_of(place, HD), HD)
-        return pltpu.make_async_copy(src.at[n], dst.at[:, lanes], store_sem.at[j, n])
-
-    def start(n, carry):
-        for j in range(2):
-            store(n, j).start()
-        return carry
-
-    def wait(n, carry):
-        for j in range(2):
-            store(n, j).wait()
-        return carry
-
-    lax.fori_loop(0, ctx_in.shape[0], start, 0)
-    for copy in plain:
+    copies = [pltpu.make_async_copy(dlat_in, dlat_out, lat_sem)]
+    parts = sems.shape[1]
+    pairs = ((ctx_in, ctx_out), (dq_in, dq_out), (dk_in, dk_out), (dv_in, dv_out))
+    for j, (src, dst) in enumerate(pairs):
+        size = src.shape[0] // parts
+        for i in range(parts):
+            rows = pl.ds(i * size, size)
+            copies.append(pltpu.make_async_copy(src.at[rows], dst.at[rows], sems.at[j, i]))
+    for copy in copies:
         copy.start()
-    lax.fori_loop(0, ctx_in.shape[0], wait, 0)
-    for copy in plain:
+    for copy in copies:
         copy.wait()
 
 
 def finish_call(context, d_queries, d_k, d_v, d_latents):
     hbm = pl.BlockSpec(memory_space=pl.ANY)
     dma = pltpu.SemaphoreType.DMA
-    steps, tokens = context.shape[:2]
-    whole = jax.ShapeDtypeStruct((tokens, steps * HD), BF16)
+    whole = jax.ShapeDtypeStruct(context.shape, BF16)
     return pl.pallas_call(
         finish_kernel,
         name="finish",
@@ -742,8 +760,8 @@
         in_specs=[hbm] * 5,
         out_specs=(hbm,) * 5,
         scratch_shapes=[
-            dma((2, steps)),
-            dma((3,)),
+            dma((4, 4)),
+            dma(()),
         ],
         compiler_params=pltpu.CompilerParams(vmem_limit_bytes=4 * 2**20),
     )(context, d_queries, d_k, d_v, d_latents)

time: 139 us -> 132 us (0.950)
  Pallas kernels: 136 us -> 130 us
    pallas_call x1, Pallas kernels: 131 us -> 126 us  [whole_call(): pl.pallas_call(whole_kernel, name='whole', out_shape=(pltpu.VMEM((tokens,...]
where the time goes in v4:
time: 132 us; the launch traced here: 131 us
  Pallas kernels  130 us (98%)
    pallas_call x1, Pallas kernels, whole_call(): pl.pallas_call(whole_kernel, name='whole', out_shape=(pltpu.VMEM((tokens,...  126 us
    pallas_call x1, Pallas kernels, finish_call(): pl.pallas_call(finish_kernel, name='finish', out_shape=(whole, whole, jax...  4.26 us

profile of v4, /device:TPU:1, one launch (start us, length us, event | category | flops | bytes accessed | tf_op | source)
XLA Modules:
  0.0 130.5 jit_solution(16432824891460012414)
XLA Ops:
  0.6 125.6 %whole.1 = (bf16[512,4096]{1,0:T(8,128)(2,1)S(1)}, bf16[512,4096]{1,0:T(8,128)(2,1)S(1)}, bf16[64,1280]{1,0:T(8,128)(2,1)S(1)}, f32[1280,256]{1,0:T(8,128)S(1)}, f32[1280,256]{1,0:T(8,128)S(1)}) custom-call(s32[1,16]{1,0:T(1,128)} %pos_ref.1, s32[1,16]{1,0:T(1,128)} %slot_ref.1, bf16[64,1280]{1,0:T(8,128)(2,1)} %bitcast.8, bf16[1280,256]{1,0:T(8,128)(2,1)} %kw_hbm.1, ...), custom_call_target="tpu_custom_call" | custom-call | tf_op jit(solution)/shard_map/whole/pallas_call | solution.py:659
  126.3 4.3 %finish.1 = (bf16[512,4096]{1,0:T(8,128)(2,1)}, bf16[512,4096]{1,0:T(8,128)(2,1)}, f32[1280,256]{1,0:T(8,128)}, f32[1280,256]{1,0:T(8,128)}, bf16[64,1280]{1,0:T(8,128)(2,1)}) custom-call(bf16[512,4096]{1,0:T(8,128)(2,1)S(1)} %get-tuple-element.15.ctx_in, bf16[512,4096]{1,0:T(8,128)(2,1)S(1)} %get-tuple-element.16.dq_in, ...), custom_call_target="tpu_custom_call" | custom-call | tf_op jit(solution)/shard_map/finish/pallas_call | solution.py:750

commit v5 on v4

--- a/solution.py
+++ b/solution.py
@@ -179,15 +179,28 @@
             lat_hbm.at[high], lat_all.at[mx, my, high], l_ss.at[1, d], l_rs.at[1, d], peer(0, d)
         )
 
-    def y_second(s, d):
-        block = lat_all.at[ring(mx, SIDE - s), my, low]
-        source = lat_hbm.at[low] if s == 0 else block
-        return remote(source, block, m_ss.at[0, s, d], m_rs.at[0, s, d], peer(0, d))
-
-    def x_second(s, d):
-        block = lat_all.at[mx, ring(my, SIDE - s), high]
-        source = lat_hbm.at[high] if s == 0 else block
-        return remote(source, block, m_ss.at[1, s, d], m_rs.at[1, s, d], peer(d, 0))
+    part_rows = LATENTS // 4
+    hops = ((0, 1, 0, 2), (0, 3, 0, 2), (1, 1, 0, 1), (3, 3, 1, 1))
+
+    def second(kind, s, hop):
+        back, d, begin, parts = hops[hop]
+        rows = pl.ds((2 * kind + begin) * part_rows, parts * part_rows)
+        x, y = ((s, back), (back, s))[kind]
+        block = lat_all.at[ring(mx, SIDE - x), ring(my, SIDE - y), rows]
+        source = lat_hbm.at[rows] if back == 0 and s == 0 else block
+        target = peer(d, 0) if kind else peer(0, d)
+        return remote(source, block, m_ss.at[kind, s, hop], m_rs.at[kind, s, hop], target)
+
+    def spread(s):
+        for hop in (0, 1):
+            for kind in range(2):
+                second(kind, s, hop).start()
+
+    def pass_on(s):
+        for hop in (0, 1):
+            for kind in range(2):
+                second(kind, s, hop).wait_recv()
+                second(kind, s, hop + 2).start()
 
     copies = [pltpu.make_async_copy(lat_hbm, lat_all.at[mx, my], in_sem.at[0])]
     for head in range(heads):
@@ -205,9 +218,7 @@
     for d in peers:
         x_first(d).start()
         y_first(d).start()
-    for d in peers:
-        y_second(0, d).start()
-        x_second(0, d).start()
+    spread(0)
 
     for i in range(SIDE):
         for j in range(2):
@@ -242,17 +253,16 @@
         seen = seen + (token >= pos_ref[0, i]).astype(jnp.int32)
     img_ref[...] = seen
 
-    for s in peers:
+    for s, settled in ((1, 0), (3, 1), (2, 3)):
         x_first(s).wait_recv()
-        for d in peers:
-            y_second(s, d).start()
         y_first(s).wait_recv()
-        for d in peers:
-            x_second(s, d).start()
-    for s in (0, *peers):
-        for d in peers:
-            y_second(s, d).wait_recv()
-            x_second(s, d).wait_recv()
+        spread(s)
+        pass_on(settled)
+    pass_on(2)
+    for s in range(SIDE):
+        for kind in range(2):
+            second(kind, s, 2).wait_recv()
+            second(kind, s, 3).wait_recv()
     for copy in copies:
         copy.wait()
 
@@ -539,7 +549,7 @@
 
         @pl.when(d > 0)
         def _():
-            for e in order[:2]:
+            for e in order[:3]:
                 da_copy(d, e).start()
 
         grads = grad_ref[:, y].reshape(group, heads * pair)
@@ -547,7 +557,7 @@
 
         @pl.when(d > 0)
         def _():
-            for e in order[:2]:
+            for e in order[:3]:
                 db_copy(d, e).start()
 
         return carry
@@ -592,7 +602,6 @@
     core_sum(1)
     hand_over(0)
     latent_step(1)
-    latent_send(2)
     z_sum(1)
     latent_step(3)
     latent_send(0)
@@ -620,8 +629,6 @@
         ea_copy(d).wait_send()
         eb_copy(d).wait_send()
         for s in (0, *peers):
-            x_second(s, d).wait_send()
-            y_second(s, d).wait_send()
             da_copy(d, s).wait_send()
             db_copy(d, s).wait_send()
         for head in range(heads):
@@ -631,6 +638,11 @@
         core_copy(head).wait_send()
         for d in range(SIDE):
             h_copy(head, d).wait_send()
+
+    for kind in range(2):
+        for hop in range(4):
+            for s in range(SIDE):
+                second(kind, s, hop).wait_send()
 
     def drain(n, carry):
         @pl.when(lax.rem(n, SEQ) > 0)

time: 132 us -> 128 us (0.970); the launches traced: 131 us -> 128 us
  Pallas kernels: 130 us -> 128 us
    pallas_call x1, Pallas kernels: 126 us -> 123 us  [whole_call(): pl.pallas_call(whole_kernel, name='whole', out_shape=(pltpu.VMEM((tokens,...]
where the time goes in v5:
time: 128 us
  Pallas kernels  128 us (100%)
    pallas_call x1, Pallas kernels, whole_call(): pl.pallas_call(whole_kernel, name='whole', out_shape=(pltpu.VMEM((tokens,...  123 us
    pallas_call x1, Pallas kernels, finish_call(): pl.pallas_call(finish_kernel, name='finish', out_shape=(whole, whole, jax...  4.26 us

profile of v5, /device:TPU:1, one launch (start us, length us, event | category | flops | bytes accessed | tf_op | source)
XLA Modules:
  0.0 128.2 jit_solution(15637894007332624670)
XLA Ops:
  0.6 123.3 %whole.1 = (bf16[512,4096]{1,0:T(8,128)(2,1)S(1)}, bf16[512,4096]{1,0:T(8,128)(2,1)S(1)}, bf16[64,1280]{1,0:T(8,128)(2,1)S(1)}, f32[1280,256]{1,0:T(8,128)S(1)}, f32[1280,256]{1,0:T(8,128)S(1)}) custom-call(s32[1,16]{1,0:T(1,128)} %pos_ref.1, s32[1,16]{1,0:T(1,128)} %slot_ref.1, bf16[64,1280]{1,0:T(8,128)(2,1)} %bitcast.8, bf16[1280,256]{1,0:T(8,128)(2,1)} %kw_hbm.1, ...), custom_call_target="tpu_custom_call" | custom-call | tf_op jit(solution)/shard_map/whole/pallas_call | solution.py:671
  123.9 4.3 %finish.1 = (bf16[512,4096]{1,0:T(8,128)(2,1)}, bf16[512,4096]{1,0:T(8,128)(2,1)}, f32[1280,256]{1,0:T(8,128)}, f32[1280,256]{1,0:T(8,128)}, bf16[64,1280]{1,0:T(8,128)(2,1)}) custom-call(bf16[512,4096]{1,0:T(8,128)(2,1)S(1)} %get-tuple-element.15.ctx_in, bf16[512,4096]{1,0:T(8,128)(2,1)S(1)} %get-tuple-element.16.dq_in, ...), custom_call_target="tpu_custom_call" | custom-call | tf_op jit(solution)/shard_map/finish/pallas_call | solution.py:762

commit v6 on v5

--- a/solution.py
+++ b/solution.py
@@ -592,16 +592,16 @@
     core_copy(0).start()
     weight_grad(0, own_rows)
     core_sum(0)
-    z_sum(0)
 
     key_value_grads(1)
     weight_grad(1, other_rows)
     core_copy(1).start()
+    z_sum(0)
     lax.fori_loop(0, SIDE, latent_grads, 0)
     weight_grad(1, own_rows)
     core_sum(1)
+    latent_step(1)
     hand_over(0)
-    latent_step(1)
     z_sum(1)
     latent_step(3)
     latent_send(0)

time: 128 us -> 128 us (level)
  no operation moved by 1% of the time
where the time goes in v6:
time: 128 us
  Pallas kernels  127 us (99%)
    pallas_call x1, Pallas kernels, whole_call(): pl.pallas_call(whole_kernel, name='whole', out_shape=(pltpu.VMEM((tokens,...  123 us
    pallas_call x1, Pallas kernels, finish_call(): pl.pallas_call(finish_kernel, name='finish', out_shape=(whole, whole, jax...  4.26 us

profile of v6, /device:TPU:1, one launch (start us, length us, event | category | flops | bytes accessed | tf_op | source)
XLA Modules:
  0.0 128.0 jit_solution(6077267764280963646)
XLA Ops:
  0.6 123.1 %whole.1 = (bf16[512,4096]{1,0:T(8,128)(2,1)S(1)}, bf16[512,4096]{1,0:T(8,128)(2,1)S(1)}, bf16[64,1280]{1,0:T(8,128)(2,1)S(1)}, f32[1280,256]{1,0:T(8,128)S(1)}, f32[1280,256]{1,0:T(8,128)S(1)}) custom-call(s32[1,16]{1,0:T(1,128)} %pos_ref.1, s32[1,16]{1,0:T(1,128)} %slot_ref.1, bf16[64,1280]{1,0:T(8,128)(2,1)} %bitcast.8, bf16[1280,256]{1,0:T(8,128)(2,1)} %kw_hbm.1, ...), custom_call_target="tpu_custom_call" | custom-call | tf_op jit(solution)/shard_map/whole/pallas_call | solution.py:671
  123.8 4.3 %finish.1 = (bf16[512,4096]{1,0:T(8,128)(2,1)}, bf16[512,4096]{1,0:T(8,128)(2,1)}, f32[1280,256]{1,0:T(8,128)}, f32[1280,256]{1,0:T(8,128)}, bf16[64,1280]{1,0:T(8,128)(2,1)}) custom-call(bf16[512,4096]{1,0:T(8,128)(2,1)S(1)} %get-tuple-element.15.ctx_in, bf16[512,4096]{1,0:T(8,128)(2,1)S(1)} %get-tuple-element.16.dq_in, ...), custom_call_target="tpu_custom_call" | custom-call | tf_op jit(solution)/shard_map/finish/pallas_call | solution.py:762
